TPU v7x, 512 devices: a whole 4x8x8 slice. The times are simulated.
512 devices in a mesh: gz: 32 (over x_lo, z, core), gx: 16 (over y, x_hi).
Axes of the slice: x: 4 (x_hi: 2, x_lo: 2; x = x_hi * 2 + x_lo), y: 8, z: 8, core: 2. Of those that a mesh axis runs over, the one named last changes fastest.
Arguments:
- image: bfloat16 [32, 256, 5120], P('gz', None, 'gx'), may hold values from -200 to 200, as said below
- flags: int32 [32, 2], P('gz'), may hold values 0 or 1
- offsets: int32 [32, 1, 128, 2], P('gz', None, 'gx'), may hold values from -40 to 40
Outputs:
- corr_near: float32 [32, 1, 128, 128, 128], P('gz', None, 'gx')
- corr_far: float32 [32, 1, 128, 128, 128], P('gz', None, 'gx')
Inputs may be any that keep to these rules, and one draw needn't show every extreme that they name: `image`: pixel intensities.
All inputs are finite; a program needn't handle non-finite values. No bound on the sum of `flags` on one device may be relied on, other than what follows from the above.
Results may differ from a plain program's by a relative error of at most 0.009.
Values may be sent and summed in bfloat16 or wider, within the bound.
A program may use at most 64 MiB of HBM per device.

v0:
```python
import math

import jax
import jax.numpy as jnp
from jax import lax
from jax.sharding import PartitionSpec as P

P_SIZE = 256
STRIDE = 40
OFFMAX = 40
CROP = 128


def shifted(block, axis, distance):
    devices = range(lax.axis_size(axis))
    route = [(i - distance, i) for i in devices if i - distance in devices]
    return lax.ppermute(block, axis, route)


def extended(block, sides, width):
    for axis, dim in sides:
        count = lax.axis_size(axis)
        forward = [(i, i + 1) for i in range(count - 1)]
        backward = [(target, source) for source, target in forward]
        low = lax.ppermute(
            lax.slice_in_dim(block, block.shape[dim] - width, None, axis=dim), axis, forward
        )
        high = lax.ppermute(lax.slice_in_dim(block, 0, width, axis=dim), axis, backward)
        block = jnp.concatenate([low, block, high], axis=dim)
    return block


def tables(index, size):
    grid = jnp.arange(size, dtype=jnp.int32)
    phase = index[:, None] * grid[None, :] % size
    angle = phase.astype(jnp.float32) * (2.0 * math.pi / size)
    return (jnp.cos(angle).astype(jnp.bfloat16), jnp.sin(angle).astype(jnp.bfloat16))


def normalize(patches):
    values = patches.astype(jnp.float32)
    centred = values - jnp.mean(values, axis=(1, 2), keepdims=True)
    factor = lax.rsqrt(jnp.mean(centred * centred, axis=(1, 2), keepdims=True) + 1e-05)
    return (centred * factor).astype(jnp.bfloat16)


def spectrum(normed, cos_f, sin_f):
    count = normed.shape[0]
    first = jnp.concatenate([cos_f, -sin_f], axis=1)
    rowwise = jnp.dot(
        normed.reshape(count * P_SIZE, P_SIZE), first, preferred_element_type=jnp.float32
    )
    rowwise = rowwise.astype(jnp.bfloat16).reshape(count, P_SIZE, 2 * P_SIZE)
    swapped = jnp.concatenate([rowwise[:, :, P_SIZE:], -rowwise[:, :, :P_SIZE]], axis=2)
    part_one = jnp.einsum("ly,byk->blk", cos_f, rowwise, preferred_element_type=jnp.float32)
    part_two = jnp.einsum("ly,byk->blk", sin_f, swapped, preferred_element_type=jnp.float32)
    return part_one + part_two


def correlate(first_spec, second_spec, cos_c, sin_c):
    scale = 1.0 / (P_SIZE * P_SIZE)
    a_re, a_im = (first_spec[:, :, :P_SIZE], first_spec[:, :, P_SIZE:])
    b_re, b_im = (second_spec[:, :, :P_SIZE], second_spec[:, :, P_SIZE:])
    cross_re = ((a_re * b_re + a_im * b_im) * scale).astype(jnp.bfloat16)
    cross_im = ((a_re * b_im - a_im * b_re) * scale).astype(jnp.bfloat16)
    cross = jnp.concatenate([cross_re, cross_im], axis=2)
    swapped = jnp.concatenate([-cross_im, cross_re], axis=2)
    inner = jnp.einsum("ul,blk->buk", cos_c, cross, preferred_element_type=jnp.float32)
    inner = inner + jnp.einsum("ul,blk->buk", sin_c, swapped, preferred_element_type=jnp.float32)
    inner = inner.astype(jnp.bfloat16)
    back = jnp.concatenate([cos_c, -sin_c], axis=1)
    return jnp.einsum("buk,vk->bvu", inner, back, preferred_element_type=jnp.float32) / P_SIZE


def cut_patches(section_cols, row_start, col_start):
    return jax.vmap(
        lambda top, left: lax.dynamic_slice(section_cols, (left, top), (P_SIZE, P_SIZE))
    )(row_start, col_start)


def neighbours(base):
    near = shifted(base, "gz", -1)
    far = shifted(base, "gz", -2)
    return (near, far)


def on_device(image, flags, offsets):
    margin = P_SIZE - STRIDE + OFFMAX
    strip = jnp.transpose(image[0])
    own_ext = extended(strip, (("gx", 0),), margin)
    near_ext, far_ext = neighbours(own_ext)
    prow_count = offsets.shape[1]
    pcol_count = offsets.shape[2]
    count = prow_count * pcol_count
    cos_f, sin_f = tables(jnp.arange(P_SIZE, dtype=jnp.int32), P_SIZE)
    cos_c, sin_c = tables((jnp.arange(CROP, dtype=jnp.int32) - CROP // 2) % P_SIZE, P_SIZE)
    row_start = jnp.repeat(jnp.arange(prow_count, dtype=jnp.int32) * STRIDE, pcol_count)
    col_start = jnp.tile(margin + jnp.arange(pcol_count, dtype=jnp.int32) * STRIDE, prow_count)
    moves = offsets[0].reshape(count, 2)
    own_spec = spectrum(normalize(cut_patches(own_ext, row_start, col_start)), cos_f, sin_f)
    near_spec = spectrum(
        normalize(cut_patches(near_ext, row_start, col_start + moves[:, 0])), cos_f, sin_f
    )
    first = correlate(own_spec, near_spec, cos_c, sin_c) * flags[0, 0].astype(jnp.float32)
    far_spec = spectrum(
        normalize(cut_patches(far_ext, row_start, col_start + moves[:, 1])), cos_f, sin_f
    )
    second = correlate(own_spec, far_spec, cos_c, sin_c) * flags[0, 1].astype(jnp.float32)
    corr_near = first.reshape(1, prow_count, pcol_count, CROP, CROP)
    corr_far = second.reshape(1, prow_count, pcol_count, CROP, CROP)
    return (corr_near, corr_far)


def solution(mesh):
    in_specs = (P("gz", None, "gx"), P("gz", None), P("gz", None, "gx", None))
    out_specs = (P("gz", None, "gx", None, None), P("gz", None, "gx", None, None))
    return jax.shard_map(
        on_device, mesh=mesh, in_specs=in_specs, out_specs=out_specs, check_vma=False
    )
```

profile of v0, /device:TPU:35, one launch (start us, length us, event | category | flops | bytes accessed | tf_op | source)
XLA Modules:
  0.0 144.4 jit_solution(14388868552571204964)
XLA Ops:
  0.6 1.0 fusion.155
  1.6 3.8 %collective-permute-start = (bf16[256,256]{1,0:T(8,128)(2,1)S(1)}, bf16[256,256]{1,0:T(8,128)(2,1)S(1)}, u32[]{:S(2)}, u32[]{:S(2)}) collective-permute-start(bf16[256,256]{1,0:T(8,128)(2,1)S(1)} %get-tuple-element.64), channel_id=1, source_target_pairs={{0,1},{1,2},{2,3},{3,4},{4,5},{5,6},{6,7},{7,8},{8,9},{9,10},{10,1... | collective-permute-start | bytes 393224 | tf_op jit(solution)/shard_map/ppermute | solution.py:25
  5.4 5.1 %collective-permute-start.1 = (bf16[256,256]{1,0:T(8,128)(2,1)S(1)}, bf16[256,256]{1,0:T(8,128)(2,1)S(1)}, u32[]{:S(2)}, u32[]{:S(2)}) collective-permute-start(bf16[256,256]{1,0:T(8,128)(2,1)S(1)} %get-tuple-element.65), channel_id=1, source_target_pairs={{1,0},{2,1},{3,2},{4,3},{5,4},{6,5},{7,6},{8,7},{9,8},{10,9},{11,1... | collective-permute-start | bytes 393224 | tf_op jit(solution)/shard_map/ppermute | solution.py:28
  10.5 1.0 cosine_convert_fusion
  12.7 0.8 compare_select_fusion
  13.5 1.3 fusion.156
  16.1 1.0 fusion.77
  17.1 1.7 %pad_maximum_fusion = bf16[832,256]{1,0:T(8,128)(2,1)} fusion(bf16[256,256]{1,0:T(8,128)(2,1)S(1)} %collective-permute-done.1, bf16[320,256]{1,0:T(8,128)(2,1)} %bitcast.139, bf16[256,256]{1,0:T(8,128)(2,1)S(1)} %collective-permute-done), kind=kLoop, calls=%fused_computation.66 | loop fusion | flops 1277952 | bytes 851968 | tf_op jit(solution)/shard_map/concatenate | solution.py:29
  18.8 3.1 %collective-permute-start.2 = (bf16[832,256]{1,0:T(8,128)(2,1)}, bf16[832,256]{1,0:T(8,128)(2,1)}, u32[]{:S(2)}, u32[]{:S(2)}) collective-permute-start(bf16[832,256]{1,0:T(8,128)(2,1)} %pad_maximum_fusion), channel_id=1, source_target_pairs={{16,0},{32,16},{48,32},{64,48},{80,64},{96,80},{112,96},{128,112},... | collective-permute-start | bytes 1277960 | tf_op jit(solution)/shard_map/ppermute | solution.py:17
  22.0 10.8 %collective-permute-start.3 = (bf16[832,256]{1,0:T(8,128)(2,1)}, bf16[832,256]{1,0:T(8,128)(2,1)}, u32[]{:S(2)}, u32[]{:S(2)}) collective-permute-start(bf16[832,256]{1,0:T(8,128)(2,1)} %pad_maximum_fusion), channel_id=1, source_target_pairs={{32,0},{48,16},{64,32},{80,48},{96,64},{112,80},{128,96},{144,112}... | collective-permute-start | bytes 1277960 | tf_op jit(solution)/shard_map/ppermute | solution.py:17
  32.9 16.8 %while.3 = (s32[]{:T(128)}, bf16[832,256]{1,0:T(8,128)(2,1)}, s32[8,2]{0,1:T(2,128)S(1)}, bf16[8,256,256]{2,1,0:T(8,128)(2,1)S(1)}, s32[]{:T(128)}) while((s32[]{:T(128)}, bf16[832,256]{1,0:T(8,128)(2,1)}, s32[8,2]{0,1:T(2,128)S(1)}, bf16[8,256,256]{2,1,0:T(8,128)(2,1)S(1)}, s32[]{:T(128)}) %tuple.56), condition=%wide.while_cond, body=%wide.while_body.sunk | while | flops 2 | bytes 262241 | solution.py:77
  33.5 1.5 %bitcast_dynamic-update-slice_fusion.6 = bf16[8,256,256]{2,1,0:T(8,128)(2,1)S(1)} fusion(bf16[8,256,256]{2,1,0:T(8,128)(2,1)S(1)} %get-tuple-element.168, s32[]{:T(128)} %get-tuple-element.165, bf16[832,256]{1,0:T(8,128)(2,1)} %get-tuple-element.171, s32[]{:T(128)} %bitcast.127), kind=kLoop, calls=%fused_computation.clone.1 | loop fusion | bytes 262152 | tf_op jit(solution)/shard_map/vmap()/gather
  35.6 1.5 %bitcast_dynamic-update-slice_fusion.6 = bf16[8,256,256]{2,1,0:T(8,128)(2,1)S(1)} fusion(bf16[8,256,256]{2,1,0:T(8,128)(2,1)S(1)} %get-tuple-element.168, s32[]{:T(128)} %get-tuple-element.165, bf16[832,256]{1,0:T(8,128)(2,1)} %get-tuple-element.171, s32[]{:T(128)} %bitcast.127), kind=kLoop, calls=%fused_computation.clone.1 | loop fusion | bytes 262152 | tf_op jit(solution)/shard_map/vmap()/gather
  37.7 1.5 %bitcast_dynamic-update-slice_fusion.6 = bf16[8,256,256]{2,1,0:T(8,128)(2,1)S(1)} fusion(bf16[8,256,256]{2,1,0:T(8,128)(2,1)S(1)} %get-tuple-element.168, s32[]{:T(128)} %get-tuple-element.165, bf16[832,256]{1,0:T(8,128)(2,1)} %get-tuple-element.171, s32[]{:T(128)} %bitcast.127), kind=kLoop, calls=%fused_computation.clone.1 | loop fusion | bytes 262152 | tf_op jit(solution)/shard_map/vmap()/gather
  39.8 1.5 %bitcast_dynamic-update-slice_fusion.6 = bf16[8,256,256]{2,1,0:T(8,128)(2,1)S(1)} fusion(bf16[8,256,256]{2,1,0:T(8,128)(2,1)S(1)} %get-tuple-element.168, s32[]{:T(128)} %get-tuple-element.165, bf16[832,256]{1,0:T(8,128)(2,1)} %get-tuple-element.171, s32[]{:T(128)} %bitcast.127), kind=kLoop, calls=%fused_computation.clone.1 | loop fusion | bytes 262152 | tf_op jit(solution)/shard_map/vmap()/gather
  41.9 1.5 %bitcast_dynamic-update-slice_fusion.6 = bf16[8,256,256]{2,1,0:T(8,128)(2,1)S(1)} fusion(bf16[8,256,256]{2,1,0:T(8,128)(2,1)S(1)} %get-tuple-element.168, s32[]{:T(128)} %get-tuple-element.165, bf16[832,256]{1,0:T(8,128)(2,1)} %get-tuple-element.171, s32[]{:T(128)} %bitcast.127), kind=kLoop, calls=%fused_computation.clone.1 | loop fusion | bytes 262152 | tf_op jit(solution)/shard_map/vmap()/gather
  44.0 1.5 %bitcast_dynamic-update-slice_fusion.6 = bf16[8,256,256]{2,1,0:T(8,128)(2,1)S(1)} fusion(bf16[8,256,256]{2,1,0:T(8,128)(2,1)S(1)} %get-tuple-element.168, s32[]{:T(128)} %get-tuple-element.165, bf16[832,256]{1,0:T(8,128)(2,1)} %get-tuple-element.171, s32[]{:T(128)} %bitcast.127), kind=kLoop, calls=%fused_computation.clone.1 | loop fusion | bytes 262152 | tf_op jit(solution)/shard_map/vmap()/gather
  46.1 1.5 %bitcast_dynamic-update-slice_fusion.6 = bf16[8,256,256]{2,1,0:T(8,128)(2,1)S(1)} fusion(bf16[8,256,256]{2,1,0:T(8,128)(2,1)S(1)} %get-tuple-element.168, s32[]{:T(128)} %get-tuple-element.165, bf16[832,256]{1,0:T(8,128)(2,1)} %get-tuple-element.171, s32[]{:T(128)} %bitcast.127), kind=kLoop, calls=%fused_computation.clone.1 | loop fusion | bytes 262152 | tf_op jit(solution)/shard_map/vmap()/gather
  48.2 1.5 %bitcast_dynamic-update-slice_fusion.6 = bf16[8,256,256]{2,1,0:T(8,128)(2,1)S(1)} fusion(bf16[8,256,256]{2,1,0:T(8,128)(2,1)S(1)} %get-tuple-element.168, s32[]{:T(128)} %get-tuple-element.165, bf16[832,256]{1,0:T(8,128)(2,1)} %get-tuple-element.171, s32[]{:T(128)} %bitcast.127), kind=kLoop, calls=%fused_computation.clone.1 | loop fusion | bytes 262152 | tf_op jit(solution)/shard_map/vmap()/gather
  50.6 0.7 fusion.30
  51.4 0.7 convolution_convert_fusion.2
  52.3 3.6 %fusion.75 = f32[8,512,256]{2,1,0:T(8,128)} fusion(bf16[8,256,512]{2,1,0:T(8,128)(2,1)S(1)} %bitcast.135), kind=kOutput, calls=%fused_computation.93 | convolution fusion | flops 537853952 | bytes 6291456 | tf_op jit(solution)/shard_map/ly,byk->blk/dot_general | solution.py:55
  57.2 5.8 %add_bitcast_fusion.2 = f32[8,256,512]{1,2,0:T(8,128)} fusion(f32[8,512,256]{2,1,0:T(8,128)} %fusion.75, bf16[8,256,256]{1,2,0:T(8,128)(2,1)S(1)} %neg.26, bf16[8,256,256]{1,2,0:T(8,128)(2,1)S(1)} %copy.17), kind=kOutput, calls=%fused_computation.8 | convolution fusion | flops 543096832 | bytes 10485760 | tf_op jit(solution)/shard_map/ly,byk->blk/dot_general | solution.py:56
  63.0 18.4 %while.4 = (s32[]{:T(128)}, bf16[832,256]{1,0:T(8,128)(2,1)}, s32[8,2]{0,1:T(2,128)S(1)}, bf16[8,256,256]{2,1,0:T(8,128)(2,1)S(1)}, s32[]{:T(128)}) while((s32[]{:T(128)}, bf16[832,256]{1,0:T(8,128)(2,1)}, s32[8,2]{0,1:T(2,128)S(1)}, bf16[8,256,256]{2,1,0:T(8,128)(2,1)S(1)}, s32[]{:T(128)}) %tuple.59), condition=%wide.while_cond.1, body=%wide.while_body.1.sunk | while | flops 2 | bytes 262241 | solution.py:77
  63.1 0.6 slice.161
  63.7 1.6 %bitcast_dynamic-update-slice_fusion.7 = bf16[8,256,256]{2,1,0:T(8,128)(2,1)S(1)} fusion(bf16[8,256,256]{2,1,0:T(8,128)(2,1)S(1)} %get-tuple-element.183, s32[]{:T(128)} %get-tuple-element.180, bf16[832,256]{1,0:T(8,128)(2,1)} %get-tuple-element.186, s32[]{:T(128)} %bitcast.129), kind=kLoop, calls=%fused_computation.2.clone.1 | loop fusion | bytes 262152 | tf_op jit(solution)/shard_map/vmap()/gather
  65.4 0.6 slice.161
  66.0 1.6 %bitcast_dynamic-update-slice_fusion.7 = bf16[8,256,256]{2,1,0:T(8,128)(2,1)S(1)} fusion(bf16[8,256,256]{2,1,0:T(8,128)(2,1)S(1)} %get-tuple-element.183, s32[]{:T(128)} %get-tuple-element.180, bf16[832,256]{1,0:T(8,128)(2,1)} %get-tuple-element.186, s32[]{:T(128)} %bitcast.129), kind=kLoop, calls=%fused_computation.2.clone.1 | loop fusion | bytes 262152 | tf_op jit(solution)/shard_map/vmap()/gather
  67.7 0.6 slice.161
  68.3 1.6 %bitcast_dynamic-update-slice_fusion.7 = bf16[8,256,256]{2,1,0:T(8,128)(2,1)S(1)} fusion(bf16[8,256,256]{2,1,0:T(8,128)(2,1)S(1)} %get-tuple-element.183, s32[]{:T(128)} %get-tuple-element.180, bf16[832,256]{1,0:T(8,128)(2,1)} %get-tuple-element.186, s32[]{:T(128)} %bitcast.129), kind=kLoop, calls=%fused_computation.2.clone.1 | loop fusion | bytes 262152 | tf_op jit(solution)/shard_map/vmap()/gather
  70.0 0.6 slice.161
  70.6 1.6 %bitcast_dynamic-update-slice_fusion.7 = bf16[8,256,256]{2,1,0:T(8,128)(2,1)S(1)} fusion(bf16[8,256,256]{2,1,0:T(8,128)(2,1)S(1)} %get-tuple-element.183, s32[]{:T(128)} %get-tuple-element.180, bf16[832,256]{1,0:T(8,128)(2,1)} %get-tuple-element.186, s32[]{:T(128)} %bitcast.129), kind=kLoop, calls=%fused_computation.2.clone.1 | loop fusion | bytes 262152 | tf_op jit(solution)/shard_map/vmap()/gather
  72.9 1.6 %bitcast_dynamic-update-slice_fusion.7 = bf16[8,256,256]{2,1,0:T(8,128)(2,1)S(1)} fusion(bf16[8,256,256]{2,1,0:T(8,128)(2,1)S(1)} %get-tuple-element.183, s32[]{:T(128)} %get-tuple-element.180, bf16[832,256]{1,0:T(8,128)(2,1)} %get-tuple-element.186, s32[]{:T(128)} %bitcast.129), kind=kLoop, calls=%fused_computation.2.clone.1 | loop fusion | bytes 262152 | tf_op jit(solution)/shard_map/vmap()/gather
  75.2 1.6 %bitcast_dynamic-update-slice_fusion.7 = bf16[8,256,256]{2,1,0:T(8,128)(2,1)S(1)} fusion(bf16[8,256,256]{2,1,0:T(8,128)(2,1)S(1)} %get-tuple-element.183, s32[]{:T(128)} %get-tuple-element.180, bf16[832,256]{1,0:T(8,128)(2,1)} %get-tuple-element.186, s32[]{:T(128)} %bitcast.129), kind=kLoop, calls=%fused_computation.2.clone.1 | loop fusion | bytes 262152 | tf_op jit(solution)/shard_map/vmap()/gather
  77.5 1.6 %bitcast_dynamic-update-slice_fusion.7 = bf16[8,256,256]{2,1,0:T(8,128)(2,1)S(1)} fusion(bf16[8,256,256]{2,1,0:T(8,128)(2,1)S(1)} %get-tuple-element.183, s32[]{:T(128)} %get-tuple-element.180, bf16[832,256]{1,0:T(8,128)(2,1)} %get-tuple-element.186, s32[]{:T(128)} %bitcast.129), kind=kLoop, calls=%fused_computation.2.clone.1 | loop fusion | bytes 262152 | tf_op jit(solution)/shard_map/vmap()/gather
  79.8 1.6 %bitcast_dynamic-update-slice_fusion.7 = bf16[8,256,256]{2,1,0:T(8,128)(2,1)S(1)} fusion(bf16[8,256,256]{2,1,0:T(8,128)(2,1)S(1)} %get-tuple-element.183, s32[]{:T(128)} %get-tuple-element.180, bf16[832,256]{1,0:T(8,128)(2,1)} %get-tuple-element.186, s32[]{:T(128)} %bitcast.129), kind=kLoop, calls=%fused_computation.2.clone.1 | loop fusion | bytes 262152 | tf_op jit(solution)/shard_map/vmap()/gather
  82.3 0.7 fusion.28
  83.1 0.7 convolution_convert_fusion.1
  83.8 1.2 fusion.154
  85.0 3.6 %fusion.73 = f32[8,512,256]{2,1,0:T(8,128)} fusion(bf16[8,256,512]{2,1,0:T(8,128)(2,1)S(1)} %bitcast.137), kind=kOutput, calls=%fused_computation.91 | convolution fusion | flops 537853952 | bytes 6291456 | tf_op jit(solution)/shard_map/ly,byk->blk/dot_general | solution.py:55
  88.6 17.6 %while.5 = (s32[]{:T(128)}, bf16[832,256]{1,0:T(8,128)(2,1)}, s32[8,2]{0,1:T(2,128)S(1)}, bf16[8,256,256]{2,1,0:T(8,128)(2,1)S(1)}, s32[]{:T(128)}) while((s32[]{:T(128)}, bf16[832,256]{1,0:T(8,128)(2,1)}, s32[8,2]{0,1:T(2,128)S(1)}, bf16[8,256,256]{2,1,0:T(8,128)(2,1)S(1)}, s32[]{:T(128)}) %tuple.53), condition=%wide.while_cond.2, body=%wide.while_body.2.sunk | while | flops 2 | bytes 262241 | solution.py:77
  89.2 1.6 %bitcast_dynamic-update-slice_fusion.8 = bf16[8,256,256]{2,1,0:T(8,128)(2,1)S(1)} fusion(bf16[8,256,256]{2,1,0:T(8,128)(2,1)S(1)} %get-tuple-element.153, s32[]{:T(128)} %get-tuple-element.150, bf16[832,256]{1,0:T(8,128)(2,1)} %get-tuple-element.156, s32[]{:T(128)} %bitcast.131), kind=kLoop, calls=%fused_computation.4.clone.1 | loop fusion | bytes 262152 | tf_op jit(solution)/shard_map/vmap()/gather
  91.4 1.6 %bitcast_dynamic-update-slice_fusion.8 = bf16[8,256,256]{2,1,0:T(8,128)(2,1)S(1)} fusion(bf16[8,256,256]{2,1,0:T(8,128)(2,1)S(1)} %get-tuple-element.153, s32[]{:T(128)} %get-tuple-element.150, bf16[832,256]{1,0:T(8,128)(2,1)} %get-tuple-element.156, s32[]{:T(128)} %bitcast.131), kind=kLoop, calls=%fused_computation.4.clone.1 | loop fusion | bytes 262152 | tf_op jit(solution)/shard_map/vmap()/gather
  93.6 1.6 %bitcast_dynamic-update-slice_fusion.8 = bf16[8,256,256]{2,1,0:T(8,128)(2,1)S(1)} fusion(bf16[8,256,256]{2,1,0:T(8,128)(2,1)S(1)} %get-tuple-element.153, s32[]{:T(128)} %get-tuple-element.150, bf16[832,256]{1,0:T(8,128)(2,1)} %get-tuple-element.156, s32[]{:T(128)} %bitcast.131), kind=kLoop, calls=%fused_computation.4.clone.1 | loop fusion | bytes 262152 | tf_op jit(solution)/shard_map/vmap()/gather
  95.8 1.6 %bitcast_dynamic-update-slice_fusion.8 = bf16[8,256,256]{2,1,0:T(8,128)(2,1)S(1)} fusion(bf16[8,256,256]{2,1,0:T(8,128)(2,1)S(1)} %get-tuple-element.153, s32[]{:T(128)} %get-tuple-element.150, bf16[832,256]{1,0:T(8,128)(2,1)} %get-tuple-element.156, s32[]{:T(128)} %bitcast.131), kind=kLoop, calls=%fused_computation.4.clone.1 | loop fusion | bytes 262152 | tf_op jit(solution)/shard_map/vmap()/gather
  98.0 1.6 %bitcast_dynamic-update-slice_fusion.8 = bf16[8,256,256]{2,1,0:T(8,128)(2,1)S(1)} fusion(bf16[8,256,256]{2,1,0:T(8,128)(2,1)S(1)} %get-tuple-element.153, s32[]{:T(128)} %get-tuple-element.150, bf16[832,256]{1,0:T(8,128)(2,1)} %get-tuple-element.156, s32[]{:T(128)} %bitcast.131), kind=kLoop, calls=%fused_computation.4.clone.1 | loop fusion | bytes 262152 | tf_op jit(solution)/shard_map/vmap()/gather
  100.2 1.6 %bitcast_dynamic-update-slice_fusion.8 = bf16[8,256,256]{2,1,0:T(8,128)(2,1)S(1)} fusion(bf16[8,256,256]{2,1,0:T(8,128)(2,1)S(1)} %get-tuple-element.153, s32[]{:T(128)} %get-tuple-element.150, bf16[832,256]{1,0:T(8,128)(2,1)} %get-tuple-element.156, s32[]{:T(128)} %bitcast.131), kind=kLoop, calls=%fused_computation.4.clone.1 | loop fusion | bytes 262152 | tf_op jit(solution)/shard_map/vmap()/gather
  102.4 1.6 %bitcast_dynamic-update-slice_fusion.8 = bf16[8,256,256]{2,1,0:T(8,128)(2,1)S(1)} fusion(bf16[8,256,256]{2,1,0:T(8,128)(2,1)S(1)} %get-tuple-element.153, s32[]{:T(128)} %get-tuple-element.150, bf16[832,256]{1,0:T(8,128)(2,1)} %get-tuple-element.156, s32[]{:T(128)} %bitcast.131), kind=kLoop, calls=%fused_computation.4.clone.1 | loop fusion | bytes 262152 | tf_op jit(solution)/shard_map/vmap()/gather
  104.6 1.6 %bitcast_dynamic-update-slice_fusion.8 = bf16[8,256,256]{2,1,0:T(8,128)(2,1)S(1)} fusion(bf16[8,256,256]{2,1,0:T(8,128)(2,1)S(1)} %get-tuple-element.153, s32[]{:T(128)} %get-tuple-element.150, bf16[832,256]{1,0:T(8,128)(2,1)} %get-tuple-element.156, s32[]{:T(128)} %bitcast.131), kind=kLoop, calls=%fused_computation.4.clone.1 | loop fusion | bytes 262152 | tf_op jit(solution)/shard_map/vmap()/gather
  107.2 0.9 fusion.26
  108.1 0.7 convolution_convert_fusion
  108.8 1.6 %fusion.152 = (bf16[8,256,256]{2,1,0:T(8,128)(2,1)}, bf16[8,256,256]{2,1,0:T(8,128)(2,1)}) fusion(bf16[8,256,512]{2,1,0:T(8,128)(2,1)S(1)} %bitcast.132), kind=kLoop, calls=%fused_computation.179 | loop fusion | bytes 4194304 | tf_op jit(solution)/shard_map/slice | solution.py:54
  110.4 3.6 %fusion.71 = f32[8,512,256]{2,1,0:T(8,128)} fusion(bf16[8,256,512]{2,1,0:T(8,128)(2,1)S(1)} %bitcast.133), kind=kOutput, calls=%fused_computation.89 | convolution fusion | flops 537853952 | bytes 6291456 | tf_op jit(solution)/shard_map/ly,byk->blk/dot_general | solution.py:55
  115.2 2.3 %copy.22 = bf16[8,256,256]{1,2,0:T(8,128)(2,1)} copy(bf16[8,256,256]{2,1,0:T(8,128)(2,1)} %get-tuple-element.59) | data formatting | bytes 2097152
  117.5 1.4 neg.29
  118.9 2.3 %copy.21 = bf16[8,256,256]{1,2,0:T(8,128)(2,1)} copy(bf16[8,256,256]{2,1,0:T(8,128)(2,1)} %get-tuple-element.58) | data formatting | bytes 2097152
  121.2 4.0 %add_bitcast_fusion.1 = f32[8,256,512]{1,2,0:T(8,128)S(1)} fusion(f32[8,512,256]{2,1,0:T(8,128)} %fusion.73, bf16[8,256,256]{1,2,0:T(8,128)(2,1)S(1)} %neg.27, bf16[8,256,256]{1,2,0:T(8,128)(2,1)S(1)} %copy.19), kind=kOutput, calls=%fused_computation.7 | convolution fusion | flops 543096832 | bytes 10485760 | tf_op jit(solution)/shard_map/ly,byk->blk/dot_general | solution.py:56
  125.2 1.7 %add_bitcast_fusion = f32[8,256,512]{1,2,0:T(8,128)S(1)} fusion(f32[8,512,256]{2,1,0:T(8,128)S(1)} %copy-done.1, bf16[8,256,256]{1,2,0:T(8,128)(2,1)S(1)} %neg.29, bf16[8,256,256]{1,2,0:T(8,128)(2,1)S(1)} %copy-done.2), kind=kOutput, calls=%fused_computation.6 | convolution fusion | flops 543096832 | bytes 10485760 | tf_op jit(solution)/shard_map/ly,byk->blk/dot_general | solution.py:56
  127.4 1.3 multiply_convert_fusion.1
  128.7 2.3 %fusion.150 = (bf16[8,256,256]{1,2,0:T(8,128)(2,1)}, bf16[8,256,256]{1,2,0:T(8,128)(2,1)S(1)}, bf16[8,256,256]{1,2,0:T(8,128)(2,1)S(1)}, bf16[8,256,256]{1,2,0:T(8,128)(2,1)S(1)}) fusion(f32[8,256,512]{1,2,0:T(8,128)S(1)} %add_bitcast_fusion, f32[8,256,512]{1,2,0:T(8,128)S(1)} %copy-done, f32[8,256,512]{1,2,0:T(8,128)S(1)} %add_bitcast_fusion.1), kind=kLoop, calls=%fused_computation.177 | loop fusion | flops 6291456 | bytes 16777216 | tf_op jit(solution)/shard_map/neg | solution.py:67
  131.0 2.6 %fusion.17 = f32[8,512,128]{1,2,0:T(8,128)} fusion(bf16[8,256,256]{1,2,0:T(8,128)(2,1)S(1)} %get-tuple-element.51, bf16[8,256,256]{1,2,0:T(8,128)(2,1)S(1)} %get-tuple-element.54, s32[128]{0:T(128)S(1)} %and_select_fusion), kind=kOutput, calls=%fused_computation.29 | convolution fusion | flops 273121280 | bytes 4194816 | tf_op jit(solution)/shard_map/ul,blk->buk/dot_general | solution.py:68
  133.5 2.6 %fusion.6 = f32[8,512,128]{1,2,0:T(8,128)} fusion(bf16[8,256,256]{1,2,0:T(8,128)(2,1)S(1)} %get-tuple-element.57, bf16[8,256,256]{1,2,0:T(8,128)(2,1)S(1)} %get-tuple-element.55, s32[128]{0:T(128)S(1)} %and_select_fusion), kind=kOutput, calls=%fused_computation.18 | convolution fusion | flops 273121280 | bytes 4194816 | tf_op jit(solution)/shard_map/ul,blk->buk/dot_general | solution.py:68
  136.1 4.3 %fusion.50 = f32[1,1,8,128,128]{4,3,2,1,0:T(8,128)} fusion(f32[8,512,128]{1,2,0:T(8,128)} %fusion.17, bf16[8,256,256]{1,2,0:T(8,128)(2,1)S(1)} %get-tuple-element.54, bf16[8,256,256]{1,2,0:T(8,128)(2,1)} %get-tuple-element.50, f32[]{:T(128)} %bitcast.23, bf16[128,256]{1,0:T(8,128)(2,1)S(1)} %fusion.87, bf16[128,256]{1,0:T(8,128)(2,1)S(1)} %cosine_convert_fusion.4, ...), kind=kOutput, calls=%fused_computation.60 | convolution fusion | flops 408780800 | bytes 4850180 | tf_op jit(solution)/shard_map/buk,vk->bvu/dot_general | solution.py:72
  140.4 4.0 %fusion.56 = f32[1,1,8,128,128]{4,3,2,1,0:T(8,128)} fusion(f32[8,512,128]{1,2,0:T(8,128)} %fusion.6, bf16[8,256,256]{1,2,0:T(8,128)(2,1)S(1)} %get-tuple-element.55, bf16[8,256,256]{1,2,0:T(8,128)(2,1)S(1)} %get-tuple-element.56, f32[]{:T(128)} %bitcast.16, bf16[128,256]{1,0:T(8,128)(2,1)S(1)} %fusion.87, bf16[128,256]{1,0:T(8,128)(2,1)S(1)} %cosine_convert_fusion.4, ...), kind=kOutput, calls=%fused_computation.62 | convolution fusion | flops 408780800 | bytes 4850180 | tf_op jit(solution)/shard_map/buk,vk->bvu/dot_general | solution.py:72
  (97 shorter events, 19.5 us)
Async XLA Ops:
  1.6 15.5 %collective-permute-start = (bf16[256,256]{1,0:T(8,128)(2,1)S(1)}, bf16[256,256]{1,0:T(8,128)(2,1)S(1)}, u32[]{:S(2)}, u32[]{:S(2)}) collective-permute-start(bf16[256,256]{1,0:T(8,128)(2,1)S(1)} %get-tuple-element.64), channel_id=1, source_target_pairs={{0,1},{1,2},{2,3},{3,4},{4,5},{5,6},{6,7},{7,8},{8,9},{9,10},{10,1... | collective-permute-start | bytes 393224 | tf_op jit(solution)/shard_map/ppermute | solution.py:25
  5.4 11.7 %collective-permute-start.1 = (bf16[256,256]{1,0:T(8,128)(2,1)S(1)}, bf16[256,256]{1,0:T(8,128)(2,1)S(1)}, u32[]{:S(2)}, u32[]{:S(2)}) collective-permute-start(bf16[256,256]{1,0:T(8,128)(2,1)S(1)} %get-tuple-element.65), channel_id=1, source_target_pairs={{1,0},{2,1},{3,2},{4,3},{5,4},{6,5},{7,6},{8,7},{9,8},{10,9},{11,1... | collective-permute-start | bytes 393224 | tf_op jit(solution)/shard_map/ppermute | solution.py:28
  18.8 44.2 %collective-permute-start.2 = (bf16[832,256]{1,0:T(8,128)(2,1)}, bf16[832,256]{1,0:T(8,128)(2,1)}, u32[]{:S(2)}, u32[]{:S(2)}) collective-permute-start(bf16[832,256]{1,0:T(8,128)(2,1)} %pad_maximum_fusion), channel_id=1, source_target_pairs={{16,0},{32,16},{48,32},{64,48},{80,64},{96,80},{112,96},{128,112},... | collective-permute-start | bytes 1277960 | tf_op jit(solution)/shard_map/ppermute | solution.py:17
  22.0 66.6 %collective-permute-start.3 = (bf16[832,256]{1,0:T(8,128)(2,1)}, bf16[832,256]{1,0:T(8,128)(2,1)}, u32[]{:S(2)}, u32[]{:S(2)}) collective-permute-start(bf16[832,256]{1,0:T(8,128)(2,1)} %pad_maximum_fusion), channel_id=1, source_target_pairs={{32,0},{48,16},{64,32},{80,48},{96,64},{112,80},{128,96},{144,112}... | collective-permute-start | bytes 1277960 | tf_op jit(solution)/shard_map/ppermute | solution.py:17
  110.4 3.6 %copy-start.3 = (bf16[8,256,256]{2,1,0:T(8,128)(2,1)S(1)}, bf16[8,256,256]{2,1,0:T(8,128)(2,1)}, u32[]{:S(2)}) copy-start(bf16[8,256,256]{2,1,0:T(8,128)(2,1)} %get-tuple-element.63) | copy-start | bytes 3145732
  121.2 4.0 %copy-start.1 = (f32[8,512,256]{2,1,0:T(8,128)S(1)}, f32[8,512,256]{2,1,0:T(8,128)}, u32[]{:S(2)}) copy-start(f32[8,512,256]{2,1,0:T(8,128)} %fusion.71) | copy-start | bytes 12582916
  121.2 4.0 %copy-start.2 = (bf16[8,256,256]{1,2,0:T(8,128)(2,1)S(1)}, bf16[8,256,256]{1,2,0:T(8,128)(2,1)}, u32[]{:S(2)}) copy-start(bf16[8,256,256]{1,2,0:T(8,128)(2,1)} %copy.21) | copy-start | bytes 3145732
  125.2 2.2 %copy-start = (f32[8,256,512]{1,2,0:T(8,128)S(1)}, f32[8,256,512]{1,2,0:T(8,128)}, u32[]{:S(2)}) copy-start(f32[8,256,512]{1,2,0:T(8,128)} %add_bitcast_fusion.2) | copy-start | bytes 12582916
where the time goes:
time: 146 us; the launch traced here: 144 us
  local copies, waits for them, and re-layouts  65.4 us (45%)
  matrix products  37.9 us (26%)
  starting transfers between devices  22.9 us (16%)
  other arithmetic  15.6 us (11%)
  between operations  2.24 us (2%)
    gather x72, local copies, waits for them, and re-layouts  52.4 us
    ppermute x2, starting transfers between devices, shifted(): return lax.ppermute(block, axis, route)  14 us
    dot_general x3, matrix products, spectrum(): jnp.einsum('ly,byk->blk', sin_f, swapped, preferred_element_type=jnp.floa...  11.5 us
    dot_general x3, matrix products, spectrum(): jnp.einsum('ly,byk->blk', cos_f, rowwise, preferred_element_type=jnp.floa...  10.8 us
    dot_general x2, matrix products, correlate(): jnp.einsum('buk,vk->bvu', inner, back, preferred_element_type=jnp.float32)  8.28 us
    unnamed x29, local copies, waits for them, and re-layouts  7.74 us
    dot_general x2, matrix products, correlate(): jnp.einsum('ul,blk->buk', cos_c, cross, preferred_element_type=jnp.float32)  5.16 us
    ppermute x1, starting transfers between devices, extended(): lax.ppermute(lax.slice_in_dim(block, 0, width, axis=dim), axis, backward)  5.14 us
  transfers between devices with their start and end apart: 4, of which 0 were waited for; matrix products, arithmetic and copies ran while one was open for 42% of the time, Pallas kernels for 0%

commit v1 on v0

v1 whole, which is shorter than its diff:
```python
import jax
import jax.numpy as jnp
import numpy as np
from jax import lax
from jax.experimental import pallas as pl
from jax.experimental.pallas import tpu as pltpu
from jax.sharding import PartitionSpec as P

P_SIZE = 256
STRIDE = 40
OFFMAX = 40
CROP = 128
HALF = P_SIZE // 2
LOW = 48
HIGH = 256
MESH = pl.DeviceIdType.MESH
F32 = jnp.float32
BF16 = jnp.bfloat16


def transform_tables():
    n = np.arange(P_SIZE)
    k = np.arange(HALF)
    angle = 2.0 * np.pi / P_SIZE
    full = np.zeros((P_SIZE, P_SIZE))
    full[:HALF] = np.cos(angle * ((k[:, None] * n[None]) % P_SIZE))
    full[HALF:] = np.sin(angle * ((k[:, None] * n[None]) % P_SIZE))
    full[HALF] = 1.0 - 2.0 * (n % 2)
    shifts = (np.arange(CROP) - CROP // 2) % P_SIZE
    crop = full[:, shifts].T.copy()
    crop[:, 0] *= 0.5
    crop[:, HALF] *= 0.5
    return full.astype(jnp.bfloat16), crop.astype(jnp.bfloat16)


def rows_to_spectrum_y(ext_ref, ext_row, y_ref, y_row, count, full_ref, step=208):
    done = 0
    while done < count:
        size = min(step, count - done)
        values = lax.dot_general(
            ext_ref[ext_row + done : ext_row + done + size, :],
            full_ref[...],
            (((1,), (1,)), ((), ())),
            preferred_element_type=F32,
        )
        y_ref[0, y_row + done : y_row + done + size, :] = values[:, :HALF]
        y_ref[1, y_row + done : y_row + done + size, :] = values[:, HALF:]
        done += size


def patch_spectrum(y_ref, start, full_ref):
    lane = lax.broadcasted_iota(jnp.int32, (1, HALF), 1)
    left = y_ref[0, pl.ds(start, P_SIZE), :]
    right = y_ref[1, pl.ds(start, P_SIZE), :]
    mean = jnp.where(lane == 0, jnp.sum(left, axis=0, keepdims=True) * (1.0 / P_SIZE), 0.0)
    left = left - mean
    energy = jnp.sum(left * left + right * right, axis=0, keepdims=True)
    energy = energy * jnp.where(lane == 0, 1.0, 2.0)
    variance = jnp.sum(energy, axis=1, keepdims=True) * (1.0 / (P_SIZE * P_SIZE * P_SIZE))
    factor = lax.rsqrt(variance + 1e-5)
    values = jnp.concatenate([left.astype(BF16), right.astype(BF16)], axis=1)
    return jnp.dot(full_ref[...], values, preferred_element_type=F32), factor


def cross_rows(a, b, r_ref, row, size):
    lane0 = lax.broadcasted_iota(jnp.int32, (size, HALF), 1) == 0
    p, u, v, t = a(0, 0), a(0, 1), a(1, 0), a(1, 1)
    bp, bu, bv, bt = b(0, 0), b(0, 1), b(1, 0), b(1, 1)
    pp, vv, uu, tt = p * bp, v * bv, u * bu, t * bt
    pu = p * bu - u * bp
    vt = v * bt - t * bv
    same = uu + tt
    turn = u * bt - t * bu
    even_r = pp + vv + jnp.where(lane0, 0.0, same)
    odd_i = p * bv - v * bp + jnp.where(lane0, 0.0, turn)
    even_i = jnp.where(lane0, same, pu + vt)
    odd_r = jnp.where(lane0, turn, p * bt + t * bp - u * bv - v * bu)
    if row == 0:
        row0 = lax.broadcasted_iota(jnp.int32, (size, HALF), 0) == 0
        even_r = jnp.where(row0, pp + jnp.where(lane0, 0.0, uu), even_r)
        odd_i = jnp.where(row0, vv + jnp.where(lane0, 0.0, tt), odd_i)
        even_i = jnp.where(row0, jnp.where(lane0, uu, pu), even_i)
        odd_r = jnp.where(row0, jnp.where(lane0, tt, vt), odd_r)
    r_ref[row : row + size, 0:HALF] = even_r.astype(BF16)
    r_ref[row : row + size, HALF:P_SIZE] = even_i.astype(BF16)
    r_ref[HALF + row : HALF + row + size, 0:HALF] = odd_i.astype(BF16)
    r_ref[HALF + row : HALF + row + size, HALF:P_SIZE] = odd_r.astype(BF16)


def pair_window(own_ref, index, other_ref, r_ref, crop_ref, scale):
    size = 16
    for row in range(0, HALF, size):

        def own(part, side, row=row):
            return own_ref[index, HALF * part + row : HALF * part + row + size, HALF * side : HALF * (side + 1)]

        def other(part, side, row=row):
            return other_ref[HALF * part + row : HALF * part + row + size, HALF * side : HALF * (side + 1)]

        cross_rows(own, other, r_ref, row, size)
    inner = jnp.dot(crop_ref[...], r_ref[...], preferred_element_type=F32).astype(BF16)
    window = lax.dot_general(
        crop_ref[...], inner, (((1,), (1,)), ((), ())), preferred_element_type=F32
    )
    return window * scale


def kernel(
    depth, width, off_ref, flag_ref, image_ref, full_ref, crop_ref, near_ref, far_ref,
    own, part, y_own, y_part, spec_own, spec_part, fac_own, cross, send_sem, recv_sem,
):
    z = lax.axis_index("gz")
    s = lax.axis_index("gx")
    strip = image_ref.shape[0]
    top = LOW + strip
    total = top + HIGH
    count = off_ref.shape[0]
    odd = lax.rem(z, 2) == 1
    even = jnp.logical_not(odd)
    has_left, has_right = s > 0, s < width - 1
    sec1, sec2 = z < depth - 1, z < depth - 2
    above = z >= 2
    both = jnp.logical_and

    mid, left, right = pl.ds(LOW, strip), pl.ds(0, LOW), pl.ds(top, HIGH)
    head, tail = pl.ds(LOW, HIGH), pl.ds(top - LOW, LOW)

    def copy(src, dst, slot, where):
        return pltpu.make_async_remote_copy(
            src_ref=src, dst_ref=dst, send_sem=send_sem.at[slot], recv_sem=recv_sem.at[slot],
            device_id=where, device_id_type=MESH,
        )

    here = own.at[mid]
    near, far = part.at[0], part.at[1]
    mate = jnp.where(odd, z - 1, z + 1)
    own_right = (has_left, has_right, copy(own.at[head], own.at[right], 0, (z, s - 1)))
    own_left = (
        both(odd, has_right),
        both(odd, has_left),
        copy(own.at[tail], own.at[left], 1, (z, s + 1)),
    )
    far_mid = (above, sec2, copy(here, far.at[mid], 2, (z - 2, s)))
    far_right = (
        both(above, has_left),
        both(sec2, has_right),
        copy(own.at[head], far.at[right], 3, (z - 2, s - 1)),
    )
    far_left = (
        both(above, has_right),
        both(sec2, has_left),
        copy(own.at[tail], far.at[left], 4, (z - 2, s + 1)),
    )
    gives = jnp.logical_or(odd, sec2)
    takes = jnp.logical_or(even, sec1)

    def start(condition, what):
        @pl.when(condition)
        def _():
            what.start()

    def arrive(condition, what):
        @pl.when(condition)
        def _():
            what.wait_recv()

    barrier = pltpu.get_barrier_semaphore()
    senders = (
        (has_right, (z, s + 1)),
        (both(odd, has_left), (z, s - 1)),
        (sec2, (z + 2, s)),
        (both(sec2, has_right), (z + 2, s + 1)),
        (both(sec2, has_left), (z + 2, s - 1)),
        (takes, (mate, s)),
    )
    for condition, where in senders:

        @pl.when(condition)
        def _(where=where):
            pl.semaphore_signal(barrier, inc=1, device_id=where, device_id_type=MESH)

    own[LOW:top, :] = image_ref[...]
    receivers = [c[0] for c in (own_right, own_left, far_mid, far_right, far_left)] + [gives]
    pl.semaphore_wait(barrier, sum(c.astype(jnp.int32) for c in receivers))

    for sends, _, what in (far_right, own_right, far_mid, far_left, own_left):
        start(sends, what)
    near_mid = copy(here, near.at[mid], 5, (mate, s))
    near_right = copy(own.at[right], near.at[right], 6, (mate, s))
    near_left = copy(own.at[left], near.at[left], 7, (mate, s))
    pass_mid = copy(far.at[mid], near.at[mid], 5, (mate, s))
    pass_right = copy(far.at[right], near.at[right], 6, (mate, s))
    pass_left = copy(far.at[left], near.at[left], 7, (mate, s))
    start(odd, near_mid)

    def clear(condition, ref, rows):
        @pl.when(condition)
        def _():
            ref[rows, :] = jnp.zeros((rows.size, P_SIZE), BF16)

    no = jnp.logical_not
    clear(no(has_right), own, right)
    clear(no(sec2), far, mid)
    clear(no(both(sec2, has_right)), far, right)
    clear(no(both(sec2, has_left)), far, left)
    clear(no(takes), near, mid)
    clear(no(both(takes, has_right)), near, right)
    clear(no(both(takes, has_left)), near, left)

    rows_to_spectrum_y(own, LOW, y_own, 0, strip, full_ref, 160)
    arrive(*own_right[1:])
    start(both(odd, has_right), near_right)
    arrive(*own_left[1:])
    start(both(odd, has_left), near_left)
    rows_to_spectrum_y(own, top, y_own, strip, y_own.shape[1] - strip, full_ref, 224)

    def own_patch(c, carry):
        spec_own[c], factor = patch_spectrum(y_own, c * STRIDE, full_ref)
        fac_own[pl.ds(c, 1), :] = jnp.broadcast_to(factor, (1, CROP))
        return carry

    lax.fori_loop(0, count, own_patch, 0)

    def one_partner(which, middle):
        rows_to_spectrum_y(part.at[which], 0, y_part, 0, total, full_ref)
        if middle is not None:
            middle()
        flag = flag_ref[0, which].astype(F32) * (4.0 / (P_SIZE * P_SIZE * P_SIZE))

        def pair(c, carry):
            start_row = LOW + c * STRIDE + off_ref[c, which]
            spec_part[...], factor = patch_spectrum(y_part, start_row, full_ref)
            scale = fac_own[pl.ds(c, 1), :] * factor * flag
            window = pair_window(spec_own, c, spec_part, cross, crop_ref, scale)

            @pl.when(which == 0)
            def _():
                near_ref[c] = window

            @pl.when(which == 1)
            def _():
                far_ref[c] = window

            return carry

        lax.fori_loop(0, count, pair, 0)

    def wait_far(condition):
        for _, gets, what in (far_mid, far_left, far_right):
            arrive(both(condition, gets), what)

    def wait_near(condition):
        arrive(both(condition, takes), near_mid)
        arrive(both(condition, both(takes, has_left)), near_left)
        arrive(both(condition, both(takes, has_right)), near_right)

    def hand_on():
        wait_far(even)
        start(both(even, sec2), pass_mid)
        start(both(even, both(sec2, has_left)), pass_left)
        start(both(even, both(sec2, has_right)), pass_right)

    first = jnp.where(odd, 1, 0)
    wait_near(even)
    wait_far(odd)
    one_partner(first, hand_on)
    wait_near(odd)
    one_partner(1 - first, None)

    for sends, _, what in (own_right, own_left, far_mid, far_right, far_left):

        @pl.when(sends)
        def _(what=what):
            what.wait_send()

    for condition, what in (
        (gives, near_mid),
        (both(gives, has_right), near_right),
        (both(gives, has_left), near_left),
    ):

        @pl.when(condition)
        def _(what=what):
            what.wait_send()


def solution(mesh):
    depth, width = mesh.shape["gz"], mesh.shape["gx"]
    full, crop = transform_tables()

    def on_device(image, flags, offsets):
        count = offsets.shape[2]
        strip = image.shape[2]
        total = LOW + strip + HIGH
        vmem = pl.BlockSpec(memory_space=pltpu.VMEM)
        smem = pl.BlockSpec(memory_space=pltpu.SMEM)
        window = jax.ShapeDtypeStruct((count, CROP, CROP), F32)

        def body(*refs):
            kernel(depth, width, *refs)

        near, far = pl.pallas_call(
            body,
            out_shape=[window, window],
            in_specs=[smem, smem, vmem, vmem, vmem],
            out_specs=[vmem, vmem],
            scratch_shapes=[
                pltpu.VMEM((total, P_SIZE), BF16),
                pltpu.VMEM((2, total, P_SIZE), BF16),
                pltpu.VMEM((2, 544, HALF), F32),
                pltpu.VMEM((2, total, HALF), F32),
                pltpu.VMEM((count, P_SIZE, P_SIZE), F32),
                pltpu.VMEM((P_SIZE, P_SIZE), F32),
                pltpu.VMEM((count, CROP), F32),
                pltpu.VMEM((P_SIZE, P_SIZE), BF16),
                pltpu.SemaphoreType.DMA((8,)),
                pltpu.SemaphoreType.DMA((8,)),
            ],
            compiler_params=pltpu.CompilerParams(
                collective_id=0, has_side_effects=True, vmem_limit_bytes=40 * 2**20
            ),
        )(offsets.reshape(count, 2), flags, jnp.transpose(image[0]), jnp.asarray(full), jnp.asarray(crop))
        shape = (1, 1, count, CROP, CROP)
        return near.reshape(shape), far.reshape(shape)

    in_specs = (P("gz", None, "gx"), P("gz", None), P("gz", None, "gx", None))
    out_specs = (P("gz", None, "gx", None, None), P("gz", None, "gx", None, None))
    return jax.shard_map(
        on_device, mesh=mesh, in_specs=in_specs, out_specs=out_specs, check_vma=False
    )
```

time: 146 us -> 40.2 us (0.28)
  the two profiles are of different devices: /device:TPU:35 before, /device:TPU:30 now
where the time goes in v1:
time: 40.2 us; the launch traced here: 39.9 us
  Pallas kernels  33.7 us (84%)
  local copies, waits for them, and re-layouts  5.57 us (14%)
  between operations  0.65 us (2%)
    pallas_call x1, Pallas kernels, on_device(): pl.pallas_call(body, out_shape=[window, window], in_specs=[smem, smem, vm...  33.7 us
    unnamed x12, local copies, waits for them, and re-layouts  5.49 us

profile of v1, /device:TPU:30, one launch (start us, length us, event | category | flops | bytes accessed | tf_op | source)
XLA Modules:
  0.0 39.9 jit_solution(3449251285348164547)
XLA Ops:
  0.6 0.0 copy-start.4
  0.6 0.7 %copy-done.4 = s32[1,1,8,2]{2,3,1,0:T(2,128)S(1)} copy-done((s32[1,1,8,2]{2,3,1,0:T(2,128)S(1)}, s32[1,1,8,2]{2,3,1,0:T(2,128)}, u32[]{:S(2)}) %copy-start.4) | copy-done | bytes 88
  1.3 0.0 copy-start.3
  1.3 0.1 copy.7.refs_0_
  1.4 0.6 %copy-done.3 = s32[1,2]{1,0:T(1,128)S(1)} copy-done((s32[1,2]{1,0:T(1,128)S(1)}, s32[1,2]{1,0:T(1,128)}, u32[]{:S(2)}) %copy-start.3) | copy-done | bytes 32
  2.0 0.0 copy-start
  2.0 0.9 %copy-done = bf16[1,256,320]{1,2,0:T(8,128)(2,1)S(1)} copy-done((bf16[1,256,320]{1,2,0:T(8,128)(2,1)S(1)}, bf16[1,256,320]{1,2,0:T(8,128)(2,1)}, u32[]{:S(2)}) %copy-start) | copy-done | bytes 163864
  2.9 0.0 copy-start.1
  2.9 0.9 %copy-done.1 = bf16[256,256]{1,0:T(8,128)(2,1)S(1)} copy-done((bf16[256,256]{1,0:T(8,128)(2,1)S(1)}, bf16[256,256]{1,0:T(8,128)(2,1)}, u32[]{:S(2)}) %copy-start.1) | copy-done | bytes 131096
  3.8 0.0 copy-start.2
  3.8 0.8 %copy-done.2 = bf16[128,256]{1,0:T(8,128)(2,1)S(1)} copy-done((bf16[128,256]{1,0:T(8,128)(2,1)S(1)}, bf16[128,256]{1,0:T(8,128)(2,1)}, u32[]{:S(2)}) %copy-start.2) | copy-done | bytes 65560
  4.6 33.7 %shard_map.68 = (f32[8,128,128]{2,1,0:T(8,128)S(1)}, f32[8,128,128]{2,1,0:T(8,128)S(1)}) custom-call(s32[8,2]{1,0:T(8,128)S(1)} %copy.7.refs_0_, s32[1,2]{1,0:T(1,128)S(1)} %copy-done.3, bf16[320,256]{1,0:T(8,128)(2,1)S(1)} %bitcast.8, bf16[256,256]{1,0:T(8,128)(2,1)S(1)} %copy-done.1, bf16[128,256]{1,0:T(8,128)(2,1)S(1)} %copy-done.2), custom_call_target="tpu_custom_call" | custom-call | tf_op jit(solution)/shard_map/pallas_call | solution.py:302
  38.3 0.8 %copy.10 = f32[1,1,8,128,128]{4,3,2,1,0:T(8,128)} copy(f32[1,1,8,128,128]{4,3,2,1,0:T(8,128)S(1)} %bitcast.7) | data formatting | bytes 1048576
  39.1 0.8 %copy.11 = f32[1,1,8,128,128]{4,3,2,1,0:T(8,128)} copy(f32[1,1,8,128,128]{4,3,2,1,0:T(8,128)S(1)} %bitcast.6) | data formatting | bytes 1048576
Async XLA Ops:
  0.6 0.7 %copy-start.4 = (s32[1,1,8,2]{2,3,1,0:T(2,128)S(1)}, s32[1,1,8,2]{2,3,1,0:T(2,128)}, u32[]{:S(2)}) copy-start(s32[1,1,8,2]{2,3,1,0:T(2,128)} %param.7) | copy-start | bytes 196
  1.3 0.7 %copy-start.3 = (s32[1,2]{1,0:T(1,128)S(1)}, s32[1,2]{1,0:T(1,128)}, u32[]{:S(2)}) copy-start(s32[1,2]{1,0:T(1,128)} %refs_1_.1) | copy-start | bytes 28
  2.0 0.9 %copy-start = (bf16[1,256,320]{1,2,0:T(8,128)(2,1)S(1)}, bf16[1,256,320]{1,2,0:T(8,128)(2,1)}, u32[]{:S(2)}) copy-start(bf16[1,256,320]{1,2,0:T(8,128)(2,1)} %param.5) | copy-start | bytes 491524
  2.9 0.9 %copy-start.1 = (bf16[256,256]{1,0:T(8,128)(2,1)S(1)}, bf16[256,256]{1,0:T(8,128)(2,1)}, u32[]{:S(2)}) copy-start(bf16[256,256]{1,0:T(8,128)(2,1)} %constant.4.clone.refs_3_) | copy-start | bytes 393220
  3.8 0.8 %copy-start.2 = (bf16[128,256]{1,0:T(8,128)(2,1)S(1)}, bf16[128,256]{1,0:T(8,128)(2,1)}, u32[]{:S(2)}) copy-start(bf16[128,256]{1,0:T(8,128)(2,1)} %constant.5.clone.refs_4_) | copy-start | bytes 196612

commit v2 on v1

--- a/solution.py
+++ b/solution.py
@@ -87,7 +87,7 @@
     r_ref[HALF + row : HALF + row + size, HALF:P_SIZE] = odd_r.astype(BF16)
 
 
-def pair_window(own_ref, index, other_ref, r_ref, crop_ref, scale):
+def cross_power(own_ref, other_ref, index, r_ref):
     size = 16
     for row in range(0, HALF, size):
 
@@ -95,32 +95,40 @@
             return own_ref[index, HALF * part + row : HALF * part + row + size, HALF * side : HALF * (side + 1)]
 
         def other(part, side, row=row):
-            return other_ref[HALF * part + row : HALF * part + row + size, HALF * side : HALF * (side + 1)]
-
-        cross_rows(own, other, r_ref, row, size)
-    inner = jnp.dot(crop_ref[...], r_ref[...], preferred_element_type=F32).astype(BF16)
+            return other_ref[index, HALF * part + row : HALF * part + row + size, HALF * side : HALF * (side + 1)]
+
+        cross_rows(own, other, r_ref.at[index], row, size)
+
+
+def crop_window(crop_ref, r_ref, index, scale):
+    inner = jnp.dot(crop_ref[...], r_ref[index], preferred_element_type=F32).astype(BF16)
     window = lax.dot_general(
         crop_ref[...], inner, (((1,), (1,)), ((), ())), preferred_element_type=F32
     )
     return window * scale
 
 
-def kernel(
-    depth, width, off_ref, flag_ref, image_ref, full_ref, crop_ref, near_ref, far_ref,
-    own, part, y_own, y_part, spec_own, spec_part, fac_own, cross, send_sem, recv_sem,
+def exchange_kernel(
+    depth, width, off_hbm, flag_hbm, image_hbm, full_hbm, crop_hbm, window_ref, r_second, scale_second, crop_out,
+    own, part, y_own, y_part, spec_own, spec_part, r_first, full_ref, off_ref, flag_ref,
+    send_sem, recv_sem, local_sem, ready_sem,
 ):
     z = lax.axis_index("gz")
     s = lax.axis_index("gx")
-    strip = image_ref.shape[0]
+    strip = image_hbm.shape[0]
     top = LOW + strip
     total = top + HIGH
-    count = off_ref.shape[0]
+    count = off_ref.shape[1]
     odd = lax.rem(z, 2) == 1
     even = jnp.logical_not(odd)
     has_left, has_right = s > 0, s < width - 1
     sec1, sec2 = z < depth - 1, z < depth - 2
     above = z >= 2
     both = jnp.logical_and
+    no = jnp.logical_not
+    half = depth // 2
+    early = both(z >= half, z < half + 2)
+    late = both(z >= half - 2, z < half)
 
     mid, left, right = pl.ds(LOW, strip), pl.ds(0, LOW), pl.ds(top, HIGH)
     head, tail = pl.ds(LOW, HIGH), pl.ds(top - LOW, LOW)
@@ -165,26 +173,68 @@
             what.wait_recv()
 
     barrier = pltpu.get_barrier_semaphore()
-    senders = (
+    signals = (
         (has_right, (z, s + 1)),
         (both(odd, has_left), (z, s - 1)),
-        (sec2, (z + 2, s)),
-        (both(sec2, has_right), (z + 2, s + 1)),
-        (both(sec2, has_left), (z + 2, s - 1)),
         (takes, (mate, s)),
-    )
-    for condition, where in senders:
+        (both(sec2, no(late)), (z + 2, s)),
+        (both(both(sec2, no(late)), has_right), (z + 2, s + 1)),
+        (both(both(sec2, no(late)), has_left), (z + 2, s - 1)),
+        (early, (z - 2, s)),
+        (both(early, has_right), (z - 2, s + 1)),
+        (both(early, has_left), (z - 2, s - 1)),
+    )
+    for condition, where in signals:
 
         @pl.when(condition)
         def _(where=where):
             pl.semaphore_signal(barrier, inc=1, device_id=where, device_id_type=MESH)
 
-    own[LOW:top, :] = image_ref[...]
-    receivers = [c[0] for c in (own_right, own_left, far_mid, far_right, far_left)] + [gives]
-    pl.semaphore_wait(barrier, sum(c.astype(jnp.int32) for c in receivers))
-
-    for sends, _, what in (far_right, own_right, far_mid, far_left, own_left):
-        start(sends, what)
+    loads = [
+        pltpu.make_async_copy(src, dst, local_sem.at[i])
+        for i, (src, dst) in enumerate((
+            (image_hbm, here), (full_hbm, full_ref), (crop_hbm, crop_out), (off_hbm, off_ref), (flag_hbm, flag_ref)
+        ))
+    ]
+    for load in loads:
+        load.start()
+
+    def clear(condition, ref, rows):
+        @pl.when(condition)
+        def _():
+            ref[rows, :] = jnp.zeros((rows.size, P_SIZE), BF16)
+
+    clear(no(has_right), own, right)
+    clear(no(sec2), far, mid)
+    clear(no(both(sec2, has_right)), far, right)
+    clear(no(both(sec2, has_left)), far, left)
+    clear(no(takes), near, mid)
+    clear(no(both(takes, has_right)), near, right)
+    clear(no(both(takes, has_left)), near, left)
+
+    def as_int(condition):
+        return condition.astype(jnp.int32)
+
+    three = 1 + as_int(has_left) + as_int(has_right)
+    expected = as_int(has_left) + as_int(both(odd, has_right)) + as_int(gives)
+    expected += jnp.where(both(above, no(early)), three, 0) + jnp.where(late, three, 0)
+    loads[0].wait()
+    pl.semaphore_wait(barrier, expected)
+
+    for condition, where in (
+        (late, (z + 2, s)),
+        (both(late, has_right), (z + 2, s + 1)),
+        (both(late, has_left), (z + 2, s - 1)),
+    ):
+
+        @pl.when(condition)
+        def _(where=where):
+            pl.semaphore_signal(ready_sem, inc=1, device_id=where, device_id_type=MESH)
+
+    start(own_right[0], own_right[2])
+    for sends, _, what in (far_right, far_mid, far_left):
+        start(both(sends, no(early)), what)
+    start(own_left[0], own_left[2])
     near_mid = copy(here, near.at[mid], 5, (mate, s))
     near_right = copy(own.at[right], near.at[right], 6, (mate, s))
     near_left = copy(own.at[left], near.at[left], 7, (mate, s))
@@ -193,57 +243,39 @@
     pass_left = copy(far.at[left], near.at[left], 7, (mate, s))
     start(odd, near_mid)
 
-    def clear(condition, ref, rows):
-        @pl.when(condition)
-        def _():
-            ref[rows, :] = jnp.zeros((rows.size, P_SIZE), BF16)
-
-    no = jnp.logical_not
-    clear(no(has_right), own, right)
-    clear(no(sec2), far, mid)
-    clear(no(both(sec2, has_right)), far, right)
-    clear(no(both(sec2, has_left)), far, left)
-    clear(no(takes), near, mid)
-    clear(no(both(takes, has_right)), near, right)
-    clear(no(both(takes, has_left)), near, left)
-
-    rows_to_spectrum_y(own, LOW, y_own, 0, strip, full_ref, 160)
+    for load in loads[1:]:
+        load.wait()
+    rows_to_spectrum_y(own, LOW, y_own, 0, strip, full_ref, strip)
     arrive(*own_right[1:])
     start(both(odd, has_right), near_right)
     arrive(*own_left[1:])
     start(both(odd, has_left), near_left)
     rows_to_spectrum_y(own, top, y_own, strip, y_own.shape[1] - strip, full_ref, 224)
 
-    def own_patch(c, carry):
+    fac_own = []
+    for c in range(count):
         spec_own[c], factor = patch_spectrum(y_own, c * STRIDE, full_ref)
-        fac_own[pl.ds(c, 1), :] = jnp.broadcast_to(factor, (1, CROP))
-        return carry
-
-    lax.fori_loop(0, count, own_patch, 0)
-
-    def one_partner(which, middle):
-        rows_to_spectrum_y(part.at[which], 0, y_part, 0, total, full_ref)
-        if middle is not None:
-            middle()
+        fac_own.append(factor)
+
+    @pl.when(early)
+    def _():
+        pl.semaphore_wait(ready_sem, three)
+
+    for sends, _, what in (far_right, far_mid, far_left):
+        start(both(sends, early), what)
+
+    def one_partner(which, r_ref):
+        for rows, size in ((0, top), (top, HIGH)):
+            rows_to_spectrum_y(part.at[which], rows, y_part, rows, size, full_ref, 368)
         flag = flag_ref[0, which].astype(F32) * (4.0 / (P_SIZE * P_SIZE * P_SIZE))
-
-        def pair(c, carry):
-            start_row = LOW + c * STRIDE + off_ref[c, which]
-            spec_part[...], factor = patch_spectrum(y_part, start_row, full_ref)
-            scale = fac_own[pl.ds(c, 1), :] * factor * flag
-            window = pair_window(spec_own, c, spec_part, cross, crop_ref, scale)
-
-            @pl.when(which == 0)
-            def _():
-                near_ref[c] = window
-
-            @pl.when(which == 1)
-            def _():
-                far_ref[c] = window
-
-            return carry
-
-        lax.fori_loop(0, count, pair, 0)
+        scales = []
+        for c in range(count):
+            start_row = LOW + c * STRIDE + off_ref[which, c]
+            spec_part[c], factor = patch_spectrum(y_part, start_row, full_ref)
+            scales.append(jnp.broadcast_to(fac_own[c] * factor * flag, (1, CROP)))
+        for c in range(count):
+            cross_power(spec_own, spec_part, c, r_ref)
+        return scales
 
     def wait_far(condition):
         for _, gets, what in (far_mid, far_left, far_right):
@@ -254,18 +286,19 @@
         arrive(both(condition, both(takes, has_left)), near_left)
         arrive(both(condition, both(takes, has_right)), near_right)
 
-    def hand_on():
-        wait_far(even)
-        start(both(even, sec2), pass_mid)
-        start(both(even, both(sec2, has_left)), pass_left)
-        start(both(even, both(sec2, has_right)), pass_right)
-
-    first = jnp.where(odd, 1, 0)
+    wait_far(sec2)
+    start(both(even, sec2), pass_mid)
+    start(both(even, both(sec2, has_left)), pass_left)
+    start(both(even, both(sec2, has_right)), pass_right)
+    first = as_int(odd)
     wait_near(even)
-    wait_far(odd)
-    one_partner(first, hand_on)
+    scales = one_partner(first, r_first)
+    for c in range(count):
+        window_ref[c] = crop_window(crop_out, r_first, c, scales[c])
     wait_near(odd)
-    one_partner(1 - first, None)
+    scales = one_partner(1 - first, r_second)
+    for c in range(count):
+        scale_second[c : c + 1, :] = scales[c]
 
     for sends, _, what in (own_right, own_left, far_mid, far_right, far_left):
 
@@ -284,6 +317,31 @@
             what.wait_send()
 
 
+def finish_kernel(window_ref, r_ref, scale_ref, crop_ref, near_hbm, far_hbm, second, sem):
+    odd = lax.rem(lax.axis_index("gz"), 2) == 1
+    count = window_ref.shape[0]
+
+    def put(source, one, other, slot):
+        @pl.when(odd)
+        def _():
+            pltpu.make_async_copy(source, one, sem.at[slot]).start()
+
+        @pl.when(jnp.logical_not(odd))
+        def _():
+            pltpu.make_async_copy(source, other, sem.at[slot]).start()
+
+    put(window_ref, far_hbm, near_hbm, 0)
+    for c in range(count):
+        second[c] = crop_window(crop_ref, r_ref, c, scale_ref[c : c + 1, :])
+        if c % 2 == 1:
+            rows = pl.ds(c - 1, 2)
+            put(second.at[rows], near_hbm.at[rows], far_hbm.at[rows], 1 + c // 2)
+    pltpu.make_async_copy(window_ref, near_hbm, sem.at[0]).wait()
+    for c in range(1, count, 2):
+        rows = pl.ds(c - 1, 2)
+        pltpu.make_async_copy(second.at[rows], near_hbm.at[rows], sem.at[1 + c // 2]).wait()
+
+
 def solution(mesh):
     depth, width = mesh.shape["gz"], mesh.shape["gx"]
     full, crop = transform_tables()
@@ -293,33 +351,57 @@
         strip = image.shape[2]
         total = LOW + strip + HIGH
         vmem = pl.BlockSpec(memory_space=pltpu.VMEM)
-        smem = pl.BlockSpec(memory_space=pltpu.SMEM)
+        hbm = pl.BlockSpec(memory_space=pltpu.HBM)
         window = jax.ShapeDtypeStruct((count, CROP, CROP), F32)
+        spectra = jax.ShapeDtypeStruct((count, P_SIZE, P_SIZE), BF16)
+        scale = jax.ShapeDtypeStruct((count, CROP), F32)
 
         def body(*refs):
-            kernel(depth, width, *refs)
-
-        near, far = pl.pallas_call(
+            exchange_kernel(depth, width, *refs)
+
+        first, cross, scales, table = pl.pallas_call(
             body,
-            out_shape=[window, window],
-            in_specs=[smem, smem, vmem, vmem, vmem],
-            out_specs=[vmem, vmem],
+            out_shape=[window, spectra, scale, jax.ShapeDtypeStruct((CROP, P_SIZE), BF16)],
+            in_specs=[hbm] * 5,
+            out_specs=[vmem] * 4,
             scratch_shapes=[
                 pltpu.VMEM((total, P_SIZE), BF16),
                 pltpu.VMEM((2, total, P_SIZE), BF16),
                 pltpu.VMEM((2, 544, HALF), F32),
                 pltpu.VMEM((2, total, HALF), F32),
                 pltpu.VMEM((count, P_SIZE, P_SIZE), F32),
-                pltpu.VMEM((P_SIZE, P_SIZE), F32),
-                pltpu.VMEM((count, CROP), F32),
+                pltpu.VMEM((count, P_SIZE, P_SIZE), F32),
+                pltpu.VMEM((count, P_SIZE, P_SIZE), BF16),
                 pltpu.VMEM((P_SIZE, P_SIZE), BF16),
+                pltpu.SMEM((2, count), jnp.int32),
+                pltpu.SMEM((1, 2), jnp.int32),
                 pltpu.SemaphoreType.DMA((8,)),
                 pltpu.SemaphoreType.DMA((8,)),
+                pltpu.SemaphoreType.DMA((5,)),
+                pltpu.SemaphoreType.REGULAR,
             ],
+            name="exchange",
             compiler_params=pltpu.CompilerParams(
                 collective_id=0, has_side_effects=True, vmem_limit_bytes=40 * 2**20
             ),
-        )(offsets.reshape(count, 2), flags, jnp.transpose(image[0]), jnp.asarray(full), jnp.asarray(crop))
+        )(*(
+            pltpu.with_memory_space_constraint(operand, pltpu.HBM)
+            for operand in (
+                jnp.transpose(offsets[0, 0]), flags, jnp.transpose(image[0]), jnp.asarray(full), jnp.asarray(crop)
+            )
+        ))
+        near, far = pl.pallas_call(
+            finish_kernel,
+            out_shape=[window, window],
+            in_specs=[vmem] * 4,
+            out_specs=[hbm] * 2,
+            scratch_shapes=[
+                pltpu.VMEM((count, CROP, CROP), F32),
+                pltpu.SemaphoreType.DMA((1 + count // 2,)),
+            ],
+            name="finish",
+            compiler_params=pltpu.CompilerParams(vmem_limit_bytes=16 * 2**20),
+        )(first, cross, scales, table)
         shape = (1, 1, count, CROP, CROP)
         return near.reshape(shape), far.reshape(shape)
 

time: 40.2 us -> 23.5 us (0.58)
  Pallas kernels: 33.7 us -> 22.7 us
  local copies, waits for them, and re-layouts: 5.57 us -> 0 us
    pallas_call x1 -> x2, Pallas kernels: 33.7 us -> 22.7 us  [the longest x1 21.4 us: on_device(): pl.pallas_call(body, out_shape=[window, spectra, scale, jax.ShapeDtypeStr...]
    unnamed x12 -> x0, local copies, waits for them, and re-layouts: 5.49 us -> none
where the time goes in v2:
time: 23.5 us; the launch traced here: 23.3 us
  Pallas kernels  22.7 us (97%)
  between operations  0.64 us (3%)
    pallas_call x1, Pallas kernels, on_device(): pl.pallas_call(body, out_shape=[window, spectra, scale, jax.ShapeDtypeStr...  21.4 us
    pallas_call x1, Pallas kernels, on_device(): pl.pallas_call(finish_kernel, out_shape=[window, window], in_specs=[vmem]...  1.29 us

profile of v2, /device:TPU:30, one launch (start us, length us, event | category | flops | bytes accessed | tf_op | source)
XLA Modules:
  0.0 23.3 jit_solution(10326016272633344348)
XLA Ops:
  0.6 21.4 %exchange.1 = (f32[8,128,128]{2,1,0:T(8,128)S(1)}, bf16[8,256,256]{2,1,0:T(8,128)(2,1)S(1)}, f32[8,128]{1,0:T(8,128)S(1)}, bf16[128,256]{1,0:T(8,128)(2,1)S(1)}) custom-call(s32[2,8]{1,0:T(2,128)} %bitcast.9, s32[1,2]{1,0:T(1,128)} %refs_1_.1, bf16[320,256]{1,0:T(8,128)(2,1)} %bitcast.8, bf16[256,256]{1,0:T(8,128)(2,1)} %constant.4.clone.refs_3_, ...), custom_call_target="tpu_custom_call" | custom-call | tf_op jit(solution)/shard_map/exchange/pallas_call | solution.py:362
  22.1 1.3 %finish.1 = (f32[8,128,128]{2,1,0:T(8,128)}, f32[8,128,128]{2,1,0:T(8,128)}) custom-call(f32[8,128,128]{2,1,0:T(8,128)S(1)} %get-tuple-element.8.window_ref, bf16[8,256,256]{2,1,0:T(8,128)(2,1)S(1)} %get-tuple-element.9.r_ref, f32[8,128]{1,0:T(8,128)S(1)} %get-tuple-element.10.scale_ref, bf16[128,256]{1,0:T(8,128)(2,1)S(1)} %get-tuple-element.11.crop_ref), custom_call_target="tpu_custom_call" | custom-call | tf_op jit(solution)/shard_map/finish/pallas_call | solution.py:393

commit v3 on v2

--- a/solution.py
+++ b/solution.py
@@ -13,6 +13,8 @@
 HALF = P_SIZE // 2
 LOW = 48
 HIGH = 256
+INNER = (1, 2, 3)
+OUTER = (0, 4, 5, 6, 7)
 MESH = pl.DeviceIdType.MESH
 F32 = jnp.float32
 BF16 = jnp.bfloat16
@@ -110,7 +112,7 @@
 
 def exchange_kernel(
     depth, width, off_hbm, flag_hbm, image_hbm, full_hbm, crop_hbm, window_ref, r_second, scale_second, crop_out,
-    own, part, y_own, y_part, spec_own, spec_part, r_first, full_ref, off_ref, flag_ref,
+    own, part_ref, y_own, y_part, spec_own, spec_part, r_first, full_ref, off_ref, flag_ref,
     send_sem, recv_sem, local_sem, ready_sem,
 ):
     z = lax.axis_index("gz")
@@ -130,59 +132,59 @@
     early = both(z >= half, z < half + 2)
     late = both(z >= half - 2, z < half)
 
-    mid, left, right = pl.ds(LOW, strip), pl.ds(0, LOW), pl.ds(top, HIGH)
-    head, tail = pl.ds(LOW, HIGH), pl.ds(top - LOW, LOW)
-
-    def copy(src, dst, slot, where):
-        return pltpu.make_async_remote_copy(
-            src_ref=src, dst_ref=dst, send_sem=send_sem.at[slot], recv_sem=recv_sem.at[slot],
-            device_id=where, device_id_type=MESH,
-        )
-
-    here = own.at[mid]
-    near, far = part.at[0], part.at[1]
-    mate = jnp.where(odd, z - 1, z + 1)
-    own_right = (has_left, has_right, copy(own.at[head], own.at[right], 0, (z, s - 1)))
-    own_left = (
-        both(odd, has_right),
-        both(odd, has_left),
-        copy(own.at[tail], own.at[left], 1, (z, s + 1)),
-    )
-    far_mid = (above, sec2, copy(here, far.at[mid], 2, (z - 2, s)))
-    far_right = (
-        both(above, has_left),
-        both(sec2, has_right),
-        copy(own.at[head], far.at[right], 3, (z - 2, s - 1)),
-    )
-    far_left = (
-        both(above, has_right),
-        both(sec2, has_left),
-        copy(own.at[tail], far.at[left], 4, (z - 2, s + 1)),
-    )
+    here, left = pl.ds(LOW, strip), pl.ds(0, LOW)
+    low, high = pl.ds(LOW, HALF), pl.ds(LOW + HALF, strip - HALF)
+    right_a, right_b = pl.ds(top, HALF), pl.ds(top + HALF, HALF)
+    head_b, tail = pl.ds(LOW + HALF, HALF), pl.ds(top - LOW, LOW)
+    pieces = (high, low, right_a, right_b, left)
+    near, far = part_ref.at[0], part_ref.at[1]
+    mate = (jnp.where(odd, z - 1, z + 1), s)
+    before, after, back = (z, s - 1), (z, s + 1), (z - 2, s)
     gives = jnp.logical_or(odd, sec2)
     takes = jnp.logical_or(even, sec1)
 
-    def start(condition, what):
+    def copy(condition, src, rows, dst, to_rows, send_slot, recv_slot, where):
+        what = pltpu.make_async_remote_copy(
+            src_ref=src.at[rows], dst_ref=dst.at[to_rows], send_sem=send_sem.at[send_slot],
+            recv_sem=recv_sem.at[recv_slot], device_id=where, device_id_type=MESH,
+        )
+        return condition, what
+
+    own_right_a = copy(has_left, own, low, own, right_a, 0, 0, before)
+    own_right_b = copy(has_left, own, head_b, own, right_b, 1, 1, before)
+    own_left = copy(has_right, own, tail, own, left, 2, 2, after)
+    far_high = copy(above, own, high, far, high, 3, 3, back)
+    far_low = copy(above, own, low, far, low, 4, 4, back)
+    far_right_a = copy(both(above, has_right), own, right_a, far, right_a, 5, 5, back)
+    far_right_b = copy(both(sec2, has_left), far, head_b, far, right_b, 7, 6, before)
+    far_left = copy(both(sec2, has_right), far, tail, far, left, 8, 7, after)
+    beside = (True, True, has_right, has_right, has_left)
+
+    def hand(condition, source):
+        return [
+            copy(both(condition, side), source, rows, near, rows, 9 + n, 8 + n, mate)
+            for n, (rows, side) in enumerate(zip(pieces, beside))
+        ]
+
+    give_own, give_far = hand(odd, own), hand(both(even, sec2), far)
+
+    def start(what, condition=True):
+        @pl.when(both(what[0], condition))
+        def _():
+            what[1].start()
+
+    def arrive(what, condition):
         @pl.when(condition)
         def _():
-            what.start()
-
-    def arrive(condition, what):
-        @pl.when(condition)
-        def _():
-            what.wait_recv()
+            what[1].wait_recv()
 
     barrier = pltpu.get_barrier_semaphore()
     signals = (
-        (has_right, (z, s + 1)),
-        (both(odd, has_left), (z, s - 1)),
-        (takes, (mate, s)),
         (both(sec2, no(late)), (z + 2, s)),
-        (both(both(sec2, no(late)), has_right), (z + 2, s + 1)),
-        (both(both(sec2, no(late)), has_left), (z + 2, s - 1)),
-        (early, (z - 2, s)),
-        (both(early, has_right), (z - 2, s + 1)),
-        (both(early, has_left), (z - 2, s - 1)),
+        (early, back),
+        (has_right, after),
+        (has_left, before),
+        (takes, mate),
     )
     for condition, where in signals:
 
@@ -193,7 +195,7 @@
     loads = [
         pltpu.make_async_copy(src, dst, local_sem.at[i])
         for i, (src, dst) in enumerate((
-            (image_hbm, here), (full_hbm, full_ref), (crop_hbm, crop_out), (off_hbm, off_ref), (flag_hbm, flag_ref)
+            (image_hbm, own.at[here]), (full_hbm, full_ref), (crop_hbm, crop_out), (off_hbm, off_ref), (flag_hbm, flag_ref)
         ))
     ]
     for load in loads:
@@ -204,52 +206,42 @@
         def _():
             ref[rows, :] = jnp.zeros((rows.size, P_SIZE), BF16)
 
-    clear(no(has_right), own, right)
-    clear(no(sec2), far, mid)
-    clear(no(both(sec2, has_right)), far, right)
-    clear(no(both(sec2, has_left)), far, left)
-    clear(no(takes), near, mid)
-    clear(no(both(takes, has_right)), near, right)
-    clear(no(both(takes, has_left)), near, left)
+    for rows, side in zip(pieces, beside):
+        if side is not True:
+            clear(no(side), own, rows)
+        clear(no(both(sec2, side)), far, rows)
+        clear(no(both(takes, side)), near, rows)
 
     def as_int(condition):
         return condition.astype(jnp.int32)
 
-    three = 1 + as_int(has_left) + as_int(has_right)
-    expected = as_int(has_left) + as_int(both(odd, has_right)) + as_int(gives)
-    expected += jnp.where(both(above, no(early)), three, 0) + jnp.where(late, three, 0)
+    expected = as_int(has_left) + as_int(has_right) + as_int(gives)
+    expected += as_int(both(above, no(early))) + as_int(late)
     loads[0].wait()
     pl.semaphore_wait(barrier, expected)
 
-    for condition, where in (
-        (late, (z + 2, s)),
-        (both(late, has_right), (z + 2, s + 1)),
-        (both(late, has_left), (z + 2, s - 1)),
-    ):
-
-        @pl.when(condition)
-        def _(where=where):
-            pl.semaphore_signal(ready_sem, inc=1, device_id=where, device_id_type=MESH)
-
-    start(own_right[0], own_right[2])
-    for sends, _, what in (far_right, far_mid, far_left):
-        start(both(sends, no(early)), what)
-    start(own_left[0], own_left[2])
-    near_mid = copy(here, near.at[mid], 5, (mate, s))
-    near_right = copy(own.at[right], near.at[right], 6, (mate, s))
-    near_left = copy(own.at[left], near.at[left], 7, (mate, s))
-    pass_mid = copy(far.at[mid], near.at[mid], 5, (mate, s))
-    pass_right = copy(far.at[right], near.at[right], 6, (mate, s))
-    pass_left = copy(far.at[left], near.at[left], 7, (mate, s))
-    start(odd, near_mid)
+    @pl.when(late)
+    def _():
+        pl.semaphore_signal(ready_sem, inc=1, device_id=(z + 2, s), device_id_type=MESH)
+
+    start(own_right_a)
+    start(far_high, no(early))
+    start(own_right_b)
+    start(far_low, no(early))
+    start(own_left)
+    start(give_own[0])
+    start(give_own[1])
 
     for load in loads[1:]:
         load.wait()
     rows_to_spectrum_y(own, LOW, y_own, 0, strip, full_ref, strip)
-    arrive(*own_right[1:])
-    start(both(odd, has_right), near_right)
-    arrive(*own_left[1:])
-    start(both(odd, has_left), near_left)
+    arrive(own_right_a, has_right)
+    start(far_right_a, no(early))
+    start(give_own[2])
+    arrive(own_right_b, has_right)
+    start(give_own[3])
+    arrive(own_left, has_left)
+    start(give_own[4])
     rows_to_spectrum_y(own, top, y_own, strip, y_own.shape[1] - strip, full_ref, 224)
 
     fac_own = []
@@ -257,60 +249,89 @@
         spec_own[c], factor = patch_spectrum(y_own, c * STRIDE, full_ref)
         fac_own.append(factor)
 
-    @pl.when(early)
-    def _():
-        pl.semaphore_wait(ready_sem, three)
-
-    for sends, _, what in (far_right, far_mid, far_left):
-        start(both(sends, early), what)
-
-    def one_partner(which, r_ref):
-        for rows, size in ((0, top), (top, HIGH)):
-            rows_to_spectrum_y(part.at[which], rows, y_part, rows, size, full_ref, 368)
+    def to_y(which, rows, size):
+        rows_to_spectrum_y(part_ref.at[which], rows, y_part.at[which], rows, size, full_ref, 320)
+
+    def partner(which, patches, r_ref):
         flag = flag_ref[0, which].astype(F32) * (4.0 / (P_SIZE * P_SIZE * P_SIZE))
         scales = []
-        for c in range(count):
+        for c in patches:
             start_row = LOW + c * STRIDE + off_ref[which, c]
-            spec_part[c], factor = patch_spectrum(y_part, start_row, full_ref)
+            spec_part[c], factor = patch_spectrum(y_part.at[which], start_row, full_ref)
             scales.append(jnp.broadcast_to(fac_own[c] * factor * flag, (1, CROP)))
-        for c in range(count):
+        for c in patches:
             cross_power(spec_own, spec_part, c, r_ref)
         return scales
 
-    def wait_far(condition):
-        for _, gets, what in (far_mid, far_left, far_right):
-            arrive(both(condition, gets), what)
-
-    def wait_near(condition):
-        arrive(both(condition, takes), near_mid)
-        arrive(both(condition, both(takes, has_left)), near_left)
-        arrive(both(condition, both(takes, has_right)), near_right)
-
-    wait_far(sec2)
-    start(both(even, sec2), pass_mid)
-    start(both(even, both(sec2, has_left)), pass_left)
-    start(both(even, both(sec2, has_right)), pass_right)
-    first = as_int(odd)
-    wait_near(even)
-    scales = one_partner(first, r_first)
-    for c in range(count):
-        window_ref[c] = crop_window(crop_out, r_first, c, scales[c])
-    wait_near(odd)
-    scales = one_partner(1 - first, r_second)
-    for c in range(count):
-        scale_second[c : c + 1, :] = scales[c]
-
-    for sends, _, what in (own_right, own_left, far_mid, far_right, far_left):
-
-        @pl.when(sends)
-        def _(what=what):
-            what.wait_send()
-
-    for condition, what in (
-        (gives, near_mid),
-        (both(gives, has_right), near_right),
-        (both(gives, has_left), near_left),
-    ):
+    def windows(patches, scales):
+        for c, scale in zip(patches, scales):
+            window_ref[c] = crop_window(crop_out, r_first, c, scale)
+
+    def keep(scales):
+        for c in range(count):
+            scale_second[c : c + 1, :] = scales[c]
+
+    def send_late():
+        @pl.when(early)
+        def _():
+            pl.semaphore_wait(ready_sem, 1)
+
+        for what in (far_high, far_low, far_right_a):
+            start(what, early)
+
+    arrive(far_high, sec2)
+    start(far_right_b)
+    start(far_left)
+    start(give_far[0])
+    arrive(far_low, sec2)
+    start(give_far[1])
+    to_y(1, LOW, strip)
+    arrive(give_own[0], takes)
+    arrive(give_own[1], takes)
+    to_y(0, LOW, strip)
+
+    @pl.when(even)
+    def _():
+        arrive(give_own[2], has_right)
+        arrive(give_own[3], has_right)
+        arrive(give_own[4], has_left)
+        to_y(0, 0, LOW)
+        to_y(0, top, HIGH)
+        windows(range(count), partner(0, range(count), r_first))
+        send_late()
+        arrive(far_right_a, both(sec2, has_right))
+        start(give_far[2])
+        to_y(1, top, HALF)
+        arrive(far_right_b, both(sec2, has_right))
+        start(give_far[3])
+        arrive(far_left, both(sec2, has_left))
+        start(give_far[4])
+        to_y(1, 0, LOW)
+        to_y(1, top + HALF, HIGH - HALF)
+        keep(partner(1, range(count), r_second))
+
+    @pl.when(odd)
+    def _():
+        arrive(far_right_a, both(sec2, has_right))
+        to_y(1, top, HALF)
+        windows(INNER, partner(1, INNER, r_first))
+        send_late()
+        arrive(far_right_b, both(sec2, has_right))
+        arrive(far_left, both(sec2, has_left))
+        to_y(1, 0, LOW)
+        to_y(1, top + HALF, HIGH - HALF)
+        windows(OUTER, partner(1, OUTER, r_first))
+        arrive(give_far[2], both(takes, has_right))
+        arrive(give_far[3], both(takes, has_right))
+        arrive(give_far[4], both(takes, has_left))
+        to_y(0, 0, LOW)
+        to_y(0, top, HIGH)
+        keep(partner(0, range(count), r_second))
+
+    sent = [own_right_a, own_right_b, own_left, far_high, far_low, far_right_a, far_right_b, far_left]
+    for n in range(len(pieces)):
+        sent.append((jnp.logical_or(give_own[n][0], give_far[n][0]), give_own[n][1]))
+    for condition, what in sent:
 
         @pl.when(condition)
         def _(what=what):
@@ -320,26 +341,31 @@
 def finish_kernel(window_ref, r_ref, scale_ref, crop_ref, near_hbm, far_hbm, second, sem):
     odd = lax.rem(lax.axis_index("gz"), 2) == 1
     count = window_ref.shape[0]
-
-    def put(source, one, other, slot):
+    group = 2
+
+    def puts(copies):
         @pl.when(odd)
         def _():
-            pltpu.make_async_copy(source, one, sem.at[slot]).start()
+            for source, rows, slot in copies:
+                first = slot < count // group
+                pltpu.make_async_copy(source, (far_hbm if first else near_hbm).at[rows], sem.at[slot]).start()
 
         @pl.when(jnp.logical_not(odd))
         def _():
-            pltpu.make_async_copy(source, other, sem.at[slot]).start()
-
-    put(window_ref, far_hbm, near_hbm, 0)
+            for source, rows, slot in copies:
+                first = slot < count // group
+                pltpu.make_async_copy(source, (near_hbm if first else far_hbm).at[rows], sem.at[slot]).start()
+
+    rows = [pl.ds(c, group) for c in range(0, count, group)]
+    puts([(window_ref.at[r], r, n) for n, r in enumerate(rows)])
     for c in range(count):
         second[c] = crop_window(crop_ref, r_ref, c, scale_ref[c : c + 1, :])
-        if c % 2 == 1:
-            rows = pl.ds(c - 1, 2)
-            put(second.at[rows], near_hbm.at[rows], far_hbm.at[rows], 1 + c // 2)
-    pltpu.make_async_copy(window_ref, near_hbm, sem.at[0]).wait()
-    for c in range(1, count, 2):
-        rows = pl.ds(c - 1, 2)
-        pltpu.make_async_copy(second.at[rows], near_hbm.at[rows], sem.at[1 + c // 2]).wait()
+        if c % group == group - 1:
+            n = c // group
+            puts([(second.at[rows[n]], rows[n], count // group + n)])
+    for n, r in enumerate(rows):
+        pltpu.make_async_copy(window_ref.at[r], near_hbm.at[r], sem.at[n]).wait()
+        pltpu.make_async_copy(second.at[r], near_hbm.at[r], sem.at[count // group + n]).wait()
 
 
 def solution(mesh):
@@ -368,15 +394,15 @@
                 pltpu.VMEM((total, P_SIZE), BF16),
                 pltpu.VMEM((2, total, P_SIZE), BF16),
                 pltpu.VMEM((2, 544, HALF), F32),
-                pltpu.VMEM((2, total, HALF), F32),
+                pltpu.VMEM((2, 2, total, HALF), F32),
                 pltpu.VMEM((count, P_SIZE, P_SIZE), F32),
                 pltpu.VMEM((count, P_SIZE, P_SIZE), F32),
                 pltpu.VMEM((count, P_SIZE, P_SIZE), BF16),
                 pltpu.VMEM((P_SIZE, P_SIZE), BF16),
                 pltpu.SMEM((2, count), jnp.int32),
                 pltpu.SMEM((1, 2), jnp.int32),
-                pltpu.SemaphoreType.DMA((8,)),
-                pltpu.SemaphoreType.DMA((8,)),
+                pltpu.SemaphoreType.DMA((14,)),
+                pltpu.SemaphoreType.DMA((13,)),
                 pltpu.SemaphoreType.DMA((5,)),
                 pltpu.SemaphoreType.REGULAR,
             ],
@@ -397,7 +423,7 @@
             out_specs=[hbm] * 2,
             scratch_shapes=[
                 pltpu.VMEM((count, CROP, CROP), F32),
-                pltpu.SemaphoreType.DMA((1 + count // 2,)),
+                pltpu.SemaphoreType.DMA((count,)),
             ],
             name="finish",
             compiler_params=pltpu.CompilerParams(vmem_limit_bytes=16 * 2**20),

time: 23.5 us -> 22.4 us (0.953)
  the two profiles are of different devices: /device:TPU:30 before, /device:TPU:1 now
where the time goes in v3:
time: 22.4 us; the launch traced here: 22.2 us
  Pallas kernels  21.6 us (96%)
  between operations  0.64 us (3%)
    pallas_call x1, Pallas kernels, on_device(): pl.pallas_call(body, out_shape=[window, spectra, scale, jax.ShapeDtypeStr...  20.3 us
    pallas_call x1, Pallas kernels, on_device(): pl.pallas_call(finish_kernel, out_shape=[window, window], in_specs=[vmem]...  1.31 us

profile of v3, /device:TPU:1, one launch (start us, length us, event | category | flops | bytes accessed | tf_op | source)
XLA Modules:
  0.0 22.2 jit_solution(1066250992484483122)
XLA Ops:
  0.6 20.3 %exchange.1 = (f32[8,128,128]{2,1,0:T(8,128)S(1)}, bf16[8,256,256]{2,1,0:T(8,128)(2,1)S(1)}, f32[8,128]{1,0:T(8,128)S(1)}, bf16[128,256]{1,0:T(8,128)(2,1)S(1)}) custom-call(s32[2,8]{1,0:T(2,128)} %bitcast.9, s32[1,2]{1,0:T(1,128)} %refs_1_.1, bf16[320,256]{1,0:T(8,128)(2,1)} %bitcast.8, bf16[256,256]{1,0:T(8,128)(2,1)} %constant.4.clone.refs_3_, ...), custom_call_target="tpu_custom_call" | custom-call | tf_op jit(solution)/shard_map/exchange/pallas_call | solution.py:388
  20.9 1.3 %finish.1 = (f32[8,128,128]{2,1,0:T(8,128)}, f32[8,128,128]{2,1,0:T(8,128)}) custom-call(f32[8,128,128]{2,1,0:T(8,128)S(1)} %get-tuple-element.8.window_ref, bf16[8,256,256]{2,1,0:T(8,128)(2,1)S(1)} %get-tuple-element.9.r_ref, f32[8,128]{1,0:T(8,128)S(1)} %get-tuple-element.10.scale_ref, bf16[128,256]{1,0:T(8,128)(2,1)S(1)} %get-tuple-element.11.crop_ref), custom_call_target="tpu_custom_call" | custom-call | tf_op jit(solution)/shard_map/finish/pallas_call | solution.py:419

commit v4 on v3

--- a/solution.py
+++ b/solution.py
@@ -167,6 +167,9 @@
         ]
 
     give_own, give_far = hand(odd, own), hand(both(even, sec2), far)
+    pair = both(even, sec2)
+    near_right_b = copy(both(pair, has_left), far, head_b, near, right_b, 12, 11, (z + 1, s - 1))
+    near_left = copy(both(pair, has_right), far, tail, near, left, 13, 12, (z + 1, s + 1))
 
     def start(what, condition=True):
         @pl.when(both(what[0], condition))
@@ -185,6 +188,8 @@
         (has_right, after),
         (has_left, before),
         (takes, mate),
+        (both(both(odd, sec1), has_right), (z - 1, s + 1)),
+        (both(both(odd, sec1), has_left), (z - 1, s - 1)),
     )
     for condition, where in signals:
 
@@ -217,6 +222,7 @@
 
     expected = as_int(has_left) + as_int(has_right) + as_int(gives)
     expected += as_int(both(above, no(early))) + as_int(late)
+    expected += as_int(both(pair, has_left)) + as_int(both(pair, has_right))
     loads[0].wait()
     pl.semaphore_wait(barrier, expected)
 
@@ -232,9 +238,19 @@
     start(give_own[0])
     start(give_own[1])
 
+    last = both(z == 0, s == 0)
+
+    def pass_strip(condition):
+        arrive(far_high, both(condition, sec2))
+        for what in (far_right_b, near_right_b, far_left, near_left, give_far[0]):
+            start(what, condition)
+        arrive(far_low, both(condition, sec2))
+        start(give_far[1], condition)
+
     for load in loads[1:]:
         load.wait()
     rows_to_spectrum_y(own, LOW, y_own, 0, strip, full_ref, strip)
+    pass_strip(last)
     arrive(own_right_a, has_right)
     start(far_right_a, no(early))
     start(give_own[2])
@@ -279,12 +295,11 @@
         for what in (far_high, far_low, far_right_a):
             start(what, early)
 
-    arrive(far_high, sec2)
-    start(far_right_b)
-    start(far_left)
-    start(give_far[0])
-    arrive(far_low, sec2)
-    start(give_far[1])
+    def pass_on(condition):
+        arrive(far_right_a, both(condition, both(sec2, has_right)))
+        start(give_far[2], condition)
+
+    pass_strip(no(last))
     to_y(1, LOW, strip)
     arrive(give_own[0], takes)
     arrive(give_own[1], takes)
@@ -297,15 +312,13 @@
         arrive(give_own[4], has_left)
         to_y(0, 0, LOW)
         to_y(0, top, HIGH)
+        pass_on(last)
         windows(range(count), partner(0, range(count), r_first))
         send_late()
-        arrive(far_right_a, both(sec2, has_right))
-        start(give_far[2])
+        pass_on(no(last))
         to_y(1, top, HALF)
         arrive(far_right_b, both(sec2, has_right))
-        start(give_far[3])
         arrive(far_left, both(sec2, has_left))
-        start(give_far[4])
         to_y(1, 0, LOW)
         to_y(1, top + HALF, HIGH - HALF)
         keep(partner(1, range(count), r_second))
@@ -322,15 +335,15 @@
         to_y(1, top + HALF, HIGH - HALF)
         windows(OUTER, partner(1, OUTER, r_first))
         arrive(give_far[2], both(takes, has_right))
-        arrive(give_far[3], both(takes, has_right))
-        arrive(give_far[4], both(takes, has_left))
+        arrive(near_right_b, both(takes, has_right))
+        arrive(near_left, both(takes, has_left))
         to_y(0, 0, LOW)
         to_y(0, top, HIGH)
         keep(partner(0, range(count), r_second))
 
     sent = [own_right_a, own_right_b, own_left, far_high, far_low, far_right_a, far_right_b, far_left]
-    for n in range(len(pieces)):
-        sent.append((jnp.logical_or(give_own[n][0], give_far[n][0]), give_own[n][1]))
+    for n, far_give in enumerate((*give_far[:3], near_right_b, near_left)):
+        sent.append((jnp.logical_or(give_own[n][0], far_give[0]), give_own[n][1]))
     for condition, what in sent:
 
         @pl.when(condition)

time: 22.4 us -> 21.9 us (0.978)
  the two profiles are of different devices: /device:TPU:1 before, /device:TPU:473 now
where the time goes in v4:
time: 21.9 us; the launch traced here: 21.8 us
  Pallas kernels  21.1 us (96%)
  between operations  0.64 us (3%)
    pallas_call x1, Pallas kernels, on_device(): pl.pallas_call(body, out_shape=[window, spectra, scale, jax.ShapeDtypeStr...  19.8 us
    pallas_call x1, Pallas kernels, on_device(): pl.pallas_call(finish_kernel, out_shape=[window, window], in_specs=[vmem]...  1.31 us

profile of v4, /device:TPU:473, one launch (start us, length us, event | category | flops | bytes accessed | tf_op | source)
XLA Modules:
  0.0 21.8 jit_solution(833675175464230163)
XLA Ops:
  0.6 19.8 %exchange.1 = (f32[8,128,128]{2,1,0:T(8,128)S(1)}, bf16[8,256,256]{2,1,0:T(8,128)(2,1)S(1)}, f32[8,128]{1,0:T(8,128)S(1)}, bf16[128,256]{1,0:T(8,128)(2,1)S(1)}) custom-call(s32[2,8]{1,0:T(2,128)} %bitcast.9, s32[1,2]{1,0:T(1,128)} %refs_1_.1, bf16[320,256]{1,0:T(8,128)(2,1)} %bitcast.8, bf16[256,256]{1,0:T(8,128)(2,1)} %constant.4.clone.refs_3_, ...), custom_call_target="tpu_custom_call" | custom-call | tf_op jit(solution)/shard_map/exchange/pallas_call | solution.py:401
  20.4 1.3 %finish.1 = (f32[8,128,128]{2,1,0:T(8,128)}, f32[8,128,128]{2,1,0:T(8,128)}) custom-call(f32[8,128,128]{2,1,0:T(8,128)S(1)} %get-tuple-element.8.window_ref, bf16[8,256,256]{2,1,0:T(8,128)(2,1)S(1)} %get-tuple-element.9.r_ref, f32[8,128]{1,0:T(8,128)S(1)} %get-tuple-element.10.scale_ref, bf16[128,256]{1,0:T(8,128)(2,1)S(1)} %get-tuple-element.11.crop_ref), custom_call_target="tpu_custom_call" | custom-call | tf_op jit(solution)/shard_map/finish/pallas_call | solution.py:432

commit v5 on v4

--- a/solution.py
+++ b/solution.py
@@ -133,10 +133,10 @@
     late = both(z >= half - 2, z < half)
 
     here, left = pl.ds(LOW, strip), pl.ds(0, LOW)
-    low, high = pl.ds(LOW, HALF), pl.ds(LOW + HALF, strip - HALF)
+    low, high, last_rows = pl.ds(LOW, HALF), pl.ds(LOW + HALF, HALF), pl.ds(LOW + P_SIZE, strip - P_SIZE)
     right_a, right_b = pl.ds(top, HALF), pl.ds(top + HALF, HALF)
-    head_b, tail = pl.ds(LOW + HALF, HALF), pl.ds(top - LOW, LOW)
-    pieces = (high, low, right_a, right_b, left)
+    head_b, tail = high, pl.ds(top - LOW, LOW)
+    pieces = (high, low, right_a, right_b, left, last_rows)
     near, far = part_ref.at[0], part_ref.at[1]
     mate = (jnp.where(odd, z - 1, z + 1), s)
     before, after, back = (z, s - 1), (z, s + 1), (z - 2, s)
@@ -155,10 +155,11 @@
     own_left = copy(has_right, own, tail, own, left, 2, 2, after)
     far_high = copy(above, own, high, far, high, 3, 3, back)
     far_low = copy(above, own, low, far, low, 4, 4, back)
+    far_rest = copy(above, own, last_rows, far, last_rows, 6, 14, back)
     far_right_a = copy(both(above, has_right), own, right_a, far, right_a, 5, 5, back)
     far_right_b = copy(both(sec2, has_left), far, head_b, far, right_b, 7, 6, before)
     far_left = copy(both(sec2, has_right), far, tail, far, left, 8, 7, after)
-    beside = (True, True, has_right, has_right, has_left)
+    beside = (True, True, has_right, has_right, has_left, True)
 
     def hand(condition, source):
         return [
@@ -230,19 +231,24 @@
     def _():
         pl.semaphore_signal(ready_sem, inc=1, device_id=(z + 2, s), device_id_type=MESH)
 
+    start(far_high, no(early))
     start(own_right_a)
-    start(far_high, no(early))
     start(own_right_b)
+    start(far_rest, no(early))
     start(far_low, no(early))
     start(own_left)
     start(give_own[0])
     start(give_own[1])
+    start(give_own[5])
 
     last = both(z == 0, s == 0)
 
     def pass_strip(condition):
         arrive(far_high, both(condition, sec2))
-        for what in (far_right_b, near_right_b, far_left, near_left, give_far[0]):
+        for what in (far_right_b, near_right_b, give_far[0]):
+            start(what, condition)
+        arrive(far_rest, both(condition, sec2))
+        for what in (far_left, near_left, give_far[5]):
             start(what, condition)
         arrive(far_low, both(condition, sec2))
         start(give_far[1], condition)
@@ -268,15 +274,22 @@
     def to_y(which, rows, size):
         rows_to_spectrum_y(part_ref.at[which], rows, y_part.at[which], rows, size, full_ref, 320)
 
-    def partner(which, patches, r_ref):
+    def spectra(which, patches):
         flag = flag_ref[0, which].astype(F32) * (4.0 / (P_SIZE * P_SIZE * P_SIZE))
         scales = []
         for c in patches:
             start_row = LOW + c * STRIDE + off_ref[which, c]
             spec_part[c], factor = patch_spectrum(y_part.at[which], start_row, full_ref)
             scales.append(jnp.broadcast_to(fac_own[c] * factor * flag, (1, CROP)))
+        return scales
+
+    def powers(patches, r_ref):
         for c in patches:
             cross_power(spec_own, spec_part, c, r_ref)
+
+    def partner(which, patches, r_ref):
+        scales = spectra(which, patches)
+        powers(patches, r_ref)
         return scales
 
     def windows(patches, scales):
@@ -292,7 +305,7 @@
         def _():
             pl.semaphore_wait(ready_sem, 1)
 
-        for what in (far_high, far_low, far_right_a):
+        for what in (far_high, far_rest, far_low, far_right_a):
             start(what, early)
 
     def pass_on(condition):
@@ -303,6 +316,7 @@
     to_y(1, LOW, strip)
     arrive(give_own[0], takes)
     arrive(give_own[1], takes)
+    arrive(give_own[5], takes)
     to_y(0, LOW, strip)
 
     @pl.when(even)
@@ -333,16 +347,19 @@
         arrive(far_left, both(sec2, has_left))
         to_y(1, 0, LOW)
         to_y(1, top + HALF, HIGH - HALF)
-        windows(OUTER, partner(1, OUTER, r_first))
+        outer_scales = partner(1, OUTER, r_first)
         arrive(give_far[2], both(takes, has_right))
         arrive(near_right_b, both(takes, has_right))
         arrive(near_left, both(takes, has_left))
         to_y(0, 0, LOW)
         to_y(0, top, HIGH)
-        keep(partner(0, range(count), r_second))
-
-    sent = [own_right_a, own_right_b, own_left, far_high, far_low, far_right_a, far_right_b, far_left]
-    for n, far_give in enumerate((*give_far[:3], near_right_b, near_left)):
+        scales = spectra(0, range(count))
+        windows(OUTER, outer_scales)
+        powers(range(count), r_second)
+        keep(scales)
+
+    sent = [own_right_a, own_right_b, own_left, far_high, far_rest, far_low, far_right_a, far_right_b, far_left]
+    for n, far_give in enumerate((*give_far[:3], near_right_b, near_left, give_far[5])):
         sent.append((jnp.logical_or(give_own[n][0], far_give[0]), give_own[n][1]))
     for condition, what in sent:
 
@@ -414,8 +431,8 @@
                 pltpu.VMEM((P_SIZE, P_SIZE), BF16),
                 pltpu.SMEM((2, count), jnp.int32),
                 pltpu.SMEM((1, 2), jnp.int32),
-                pltpu.SemaphoreType.DMA((14,)),
-                pltpu.SemaphoreType.DMA((13,)),
+                pltpu.SemaphoreType.DMA((15,)),
+                pltpu.SemaphoreType.DMA((15,)),
                 pltpu.SemaphoreType.DMA((5,)),
                 pltpu.SemaphoreType.REGULAR,
             ],

time: 21.9 us -> 22 us (level)
  no operation moved by 1% of the time
where the time goes in v5:
time: 22 us; the launch traced here: 21.9 us
  Pallas kernels  21.2 us (96%)
  between operations  0.64 us (3%)
    pallas_call x1, Pallas kernels, on_device(): pl.pallas_call(body, out_shape=[window, spectra, scale, jax.ShapeDtypeStr...  19.9 us
    pallas_call x1, Pallas kernels, on_device(): pl.pallas_call(finish_kernel, out_shape=[window, window], in_specs=[vmem]...  1.31 us

profile of v5, /device:TPU:473, one launch (start us, length us, event | category | flops | bytes accessed | tf_op | source)
XLA Modules:
  0.0 21.9 jit_solution(18033126777081750619)
XLA Ops:
  0.6 19.9 %exchange.1 = (f32[8,128,128]{2,1,0:T(8,128)S(1)}, bf16[8,256,256]{2,1,0:T(8,128)(2,1)S(1)}, f32[8,128]{1,0:T(8,128)S(1)}, bf16[128,256]{1,0:T(8,128)(2,1)S(1)}) custom-call(s32[2,8]{1,0:T(2,128)} %bitcast.9, s32[1,2]{1,0:T(1,128)} %refs_1_.1, bf16[320,256]{1,0:T(8,128)(2,1)} %bitcast.8, bf16[256,256]{1,0:T(8,128)(2,1)} %constant.4.clone.refs_3_, ...), custom_call_target="tpu_custom_call" | custom-call | tf_op jit(solution)/shard_map/exchange/pallas_call | solution.py:418
  20.5 1.3 %finish.1 = (f32[8,128,128]{2,1,0:T(8,128)}, f32[8,128,128]{2,1,0:T(8,128)}) custom-call(f32[8,128,128]{2,1,0:T(8,128)S(1)} %get-tuple-element.8.window_ref, bf16[8,256,256]{2,1,0:T(8,128)(2,1)S(1)} %get-tuple-element.9.r_ref, f32[8,128]{1,0:T(8,128)S(1)} %get-tuple-element.10.scale_ref, bf16[128,256]{1,0:T(8,128)(2,1)S(1)} %get-tuple-element.11.crop_ref), custom_call_target="tpu_custom_call" | custom-call | tf_op jit(solution)/shard_map/finish/pallas_call | solution.py:449
